TPU v7x, 128 devices: a whole 4x4x4 slice. The times are simulated.
128 devices in a mesh: section: 16 (over x, z), tp: 8 (over y, core).
Axes of the slice: x: 4, y: 4, z: 4, core: 2. Of those that a mesh axis runs over, the one named last changes fastest.
Arguments:
- tokens: bfloat16 [8192, 8192], P('section'), may hold values from -6 to 6
- gain: float32 [8192], replicated, may hold values from 0.5 to 1.5
- q_weight: bfloat16 [8192, 4096], P(None, 'tp'), may hold values from -0.0625 to 0.0625
- q_bias: float32 [4096], P('tp'), may hold values from -14 to 14
- kv_weight: bfloat16 [8192, 2048], P(None, 'tp'), may hold values from -0.0625 to 0.0625
- kv_bias: float32 [2048], P('tp'), may hold values from -14 to 14
- out_weight: bfloat16 [4096, 8192], P('tp'), may hold values from -0.09375 to 0.09375
- placement: int32 [512, 1], replicated, may hold values from 0 to 15; in each aligned block of 32 rows (0 to 31, 32 to 63, ...) at most 4 rows name the same one
Outputs:
- mixed: bfloat16 [8192, 8192], P('section', 'tp')
- decode_cache: bfloat16 [1024, 16, 2048], P('section', None, 'tp')
Inputs may be any that keep to these rules, and one draw needn't show every extreme that they name: `placement`: within the 32 blocks of one stretch no owner is named more than 4 times.
All inputs are finite; a program needn't handle non-finite values.
Results may differ from a plain program's by a relative error of at most 0.014.
The roundings to bfloat16 on the way count: a program that leaves them out, or rounds other values in their place, can miss the bound.
Values may be sent and summed in bfloat16 or wider, within the bound.
No kernel may reach another device: no remote copies, remote signals or barrier semaphores. Data moves between devices by JAX's collectives and lax.ppermute only.
A program may use at most 256 MiB of HBM per device.

v0:
```python
import functools
import math

import jax
import jax.numpy as jnp
import numpy as np
from jax import lax
from jax.experimental import pallas as pl
from jax.experimental.pallas import tpu as pltpu
from jax.sharding import PartitionSpec as P

HD = 128
BLOCK = 16
SIDE = 4
HALF = 256
ROWS = 512
D = 8192
HEADS = 4
PAIR = 4
ROPE_BASE = 1000000.0
LOG2_SCALE = math.log2(math.e) / math.sqrt(HD)
SHARE = 256
COLS = 1024
limit = lambda mib: pltpu.CompilerParams(vmem_limit_bytes=mib * 1024 * 1024)
BF = jnp.bfloat16
F32 = jnp.float32
ANY = pl.BlockSpec(memory_space=pl.ANY)
WHOLE = pl.BlockSpec(memory_space=pltpu.VMEM)
FAR = pl.BlockSpec(memory_space=pltpu.HBM)


def tables():
    freq = ROPE_BASE ** (-(np.arange(HD // 2, dtype=np.float64) * 2.0 / HD))
    inner = np.arange(ROWS, dtype=np.float64)[:, None] * freq
    outer = ROWS * np.arange(SIDE * SIDE, dtype=np.float64)[:, None] * freq
    twice = lambda a: np.concatenate([a, a], -1)
    signed = lambda a: np.concatenate([-a, a], -1)
    small = np.concatenate([twice(np.cos(inner)), twice(np.sin(inner))], -1)
    large = np.concatenate(
        [twice(np.cos(outer)), twice(np.sin(outer)), signed(np.cos(outer)), signed(np.sin(outer))], -1
    )
    return small.astype(np.float32), large.astype(np.float32)


def angles(small, large):
    cos_r, sin_r = small[:, :HD], small[:, HD:]
    cos_s, sin_s = large[:, :HD], large[:, HD : 2 * HD]
    cos_g, sin_g = large[:, 2 * HD : 3 * HD], large[:, 3 * HD :]
    return cos_s * cos_r - sin_s * sin_r, sin_g * cos_r + cos_g * sin_r


def turn(value, cosine, sine):
    return value * cosine + pltpu.roll(value, HD // 2, 1) * sine


CHUNK = 64
GROUP = 32
DEPTH = 2048
AHEAD = 4
NORM_LIMIT = 56


def norm_kv_kernel(
    tokens, gain, weight, bias, small, large, w_out, factors, first, second, residual, w_send,
    tv, nv, wv, sv, total, st, sw, s_in, s_out
):
    chunks = ROWS // CHUNK
    rows_at = lambda i: pl.ds(pl.multiple_of(i * CHUNK, CHUNK), CHUNK)
    load = lambda i: pltpu.make_async_copy(tokens.at[rows_at(i), :], tv.at[rows_at(i), :], st.at[i])
    weights = [
        pltpu.make_async_copy(weight.at[k : k + DEPTH, :], wv.at[k : k + DEPTH, :], sw.at[k // DEPTH])
        for k in range(0, D, DEPTH)
    ]
    sibling = 1 - lax.rem(lax.axis_index("tp"), 2)
    fetches, sends = [], []
    for y in range(SIDE):
        here = pl.ds(pl.multiple_of((2 * y + sibling) * COLS, COLS), COLS)
        fetches.append(pltpu.make_async_copy(w_out.at[:, here], sv.at[y], s_in.at[y]))
        sends.append(pltpu.make_async_copy(sv.at[y], w_send.at[y], s_out.at[y]))
    for i in range(AHEAD):
        load(i).start()

    def chunk(i, _):
        load(i).wait()

        @pl.when(i < chunks - AHEAD)
        def _():
            load(i + AHEAD).start()

        for n in range(AHEAD):
            @pl.when(i == chunks - AHEAD + n)
            def _():
                weights[n].start()

        for g in range(0, CHUNK, GROUP):
            rows = pl.ds(pl.multiple_of(i * CHUNK + g, GROUP), GROUP)
            squares = jnp.zeros((GROUP, 128), F32)
            for c in range(0, D, 1024):
                wide = tv[rows, c : c + 1024].astype(F32)
                square = wide * wide
                for k in range(0, 1024, 128):
                    squares = squares + square[:, k : k + 128]
            meansq = jnp.sum(squares, axis=1, keepdims=True) * (1.0 / D)
            factor = lax.rsqrt(meansq + 1e-06)
            factors[rows, :] = jnp.broadcast_to(factor, (GROUP, 128))
            for c in range(0, D, 1024):
                wide = tv[rows, c : c + 1024].astype(F32)
                nv[rows, c : c + 1024] = (wide * factor * gain[:, c : c + 1024]).astype(BF)
        return 0

    lax.fori_loop(0, chunks, chunk, 0)
    for n in range(AHEAD, D // DEPTH):
        weights[n].start()
    for copy in fetches:
        copy.start()
    residual[...] = tv[:, pl.ds(pl.multiple_of(lax.axis_index("tp") * COLS, COLS), COLS)]
    for copy in weights:
        copy.wait()
    total[...] = jnp.dot(nv[...], wv[...], preferred_element_type=F32) + bias[...]
    for n in range(SIDE):
        fetches[n].wait()
        sends[n].start()
    cosine, sine = angles(small[...], large[pl.ds(lax.axis_index("section"), 1), :])
    keys = turn(total[:, :HD], cosine, sine).astype(BF)
    values = total[:, HD:].astype(BF)
    for half, out in enumerate((first, second)):
        rows = slice(half * HALF, (half + 1) * HALF)
        out[:, :HD] = keys[rows]
        out[:, HD:] = values[rows]
    for copy in sends:
        copy.wait()


def norm_kv(tokens, gain, weight, bias, small, large, w_out):
    half = jax.ShapeDtypeStruct((HALF, 2 * HD), BF)
    return pl.pallas_call(
        norm_kv_kernel,
        in_specs=[ANY, WHOLE, ANY, WHOLE, WHOLE, WHOLE, ANY],
        out_specs=[WHOLE] * 4 + [ANY],
        out_shape=[
            jax.ShapeDtypeStruct((ROWS, 128), F32),
            half,
            half,
            jax.ShapeDtypeStruct((ROWS, COLS), BF),
            jax.ShapeDtypeStruct((SIDE, HEADS * HD, COLS), BF),
        ],
        scratch_shapes=[
            pltpu.VMEM((ROWS, D), BF),
            pltpu.VMEM((ROWS, D), BF),
            pltpu.VMEM((D, 2 * HD), BF),
            pltpu.VMEM((SIDE, HEADS * HD, COLS), BF),
            pltpu.VMEM((ROWS, 2 * HD), F32),
            pltpu.SemaphoreType.DMA((ROWS // CHUNK,)),
            pltpu.SemaphoreType.DMA((D // DEPTH,)),
            pltpu.SemaphoreType.DMA((SIDE,)),
            pltpu.SemaphoreType.DMA((SIDE,)),
        ],
        compiler_params=limit(NORM_LIMIT),
        cost_estimate=pl.CostEstimate(flops=2 * ROWS * D * 256, bytes_accessed=20 << 20, transcendentals=0),
        name="norm_kv",
    )(tokens, gain, weight, bias, small, large, w_out)


Q_DEPTH = 1024
Q_AHEAD = 4
Q_ROWS = 256


def query_kernel(tokens, factors, gain, weight, bias, small, large, out, tv, nv, wv, total, sems):
    steps = D // Q_DEPTH
    copies = []
    for n in range(steps):
        at = slice(n * Q_DEPTH, (n + 1) * Q_DEPTH)
        copies.append(
            (
                pltpu.make_async_copy(tokens.at[:, at], tv.at[n], sems.at[n, 0]),
                pltpu.make_async_copy(weight.at[at, :], wv.at[n], sems.at[n, 1]),
            )
        )
    begin = lambda n: [copy.start() for copy in copies[n]]
    for n in range(Q_AHEAD):
        begin(n)
    total[...] = jnp.broadcast_to(bias[...], total.shape)

    def scale(n):
        for copy in copies[n]:
            copy.wait()
        if n + Q_AHEAD < steps:
            begin(n + Q_AHEAD)

    def rows_of(n, r):
        factor = factors[r : r + Q_ROWS, :1]
        at = slice(n * Q_DEPTH, (n + 1) * Q_DEPTH)
        nv[n, r : r + Q_ROWS, :] = (tv[n, r : r + Q_ROWS, :].astype(F32) * factor * gain[:, at]).astype(BF)

    scale(0)
    for r in range(0, ROWS, Q_ROWS):
        rows_of(0, r)
    for n in range(steps):
        if n + 1 < steps:
            scale(n + 1)
        for r in range(0, ROWS, Q_ROWS):
            total[r : r + Q_ROWS, :] += jnp.dot(nv[n, r : r + Q_ROWS, :], wv[n], preferred_element_type=F32)
            if n + 1 < steps:
                rows_of(n + 1, r)
    cosine, sine = angles(small[...], large[pl.ds(lax.axis_index("section"), 1), :])
    for h in range(HEADS):
        value = turn(total[:, h * HD : (h + 1) * HD], cosine, sine).astype(BF)
        for n in range(ROWS // SHARE):
            start = (n * HEADS + h) * SHARE
            out[start : start + SHARE, :] = value[n * SHARE : (n + 1) * SHARE]


def query(tokens, factors, gain, weight, bias, small, large):
    width = HEADS * HD
    steps = D // Q_DEPTH
    return pl.pallas_call(
        query_kernel,
        in_specs=[ANY, WHOLE, WHOLE, ANY, WHOLE, WHOLE, WHOLE],
        out_specs=WHOLE,
        out_shape=jax.ShapeDtypeStruct((HEADS * ROWS, HD), BF),
        scratch_shapes=[
            pltpu.VMEM((steps, ROWS, Q_DEPTH), BF),
            pltpu.VMEM((steps, ROWS, Q_DEPTH), BF),
            pltpu.VMEM((steps, Q_DEPTH, width), BF),
            pltpu.VMEM((ROWS, width), F32),
            pltpu.SemaphoreType.DMA((steps, 2)),
        ],
        compiler_params=limit(56),
        cost_estimate=pl.CostEstimate(flops=2 * ROWS * D * 512, bytes_accessed=16 << 20, transcendentals=0),
        name="query",
    )(tokens, factors, gain, weight, bias, small, large)


TILE = 128
QROWS = HEADS * ROWS


def attend(queries, keys, values, acc, maxima, rows, mask=None, first=False):
    scores = lax.dot_general(queries, keys, (((1,), (1,)), ((), ())), preferred_element_type=F32)
    if mask is not None:
        scores = jnp.where(mask, scores, -1e30)
    highest = jnp.max(scores, axis=1, keepdims=True)
    if first:
        newest = jnp.broadcast_to(highest, (rows.size, HD))
    else:
        old = maxima[rows, :]
        newest = jnp.maximum(old, highest)
        rescale = jnp.exp2((old - newest) * LOG2_SCALE)
    maxima[rows, :] = newest
    weights = jnp.exp2(scores * LOG2_SCALE - newest[:, :1] * LOG2_SCALE).astype(BF)
    added = jnp.dot(weights, values, preferred_element_type=F32)
    if first:
        acc[rows, :] = added
    else:
        acc[rows, :HD] = acc[rows, :HD] * rescale + added[:, :HD]
        acc[rows, HD:] = acc[rows, HD:] * rescale + added[:, HD:]


def attend_kernel(plan, halves, diagonal, final, staged, *refs):
    refs = list(refs)
    take = lambda n: [refs.pop(0) for _ in range(n)]
    (queries,) = take(1)
    begin = take(2)
    pieces = take(len(plan))
    placing = halves is not None
    if placing:
        (table,) = take(1)
        before = [] if diagonal else take(1)
    far_away = take(staged)
    outs = take(1 if final else 2)
    if placing:
        (cache,) = take(1)
    moves = list(zip(far_away, take(staged)))
    if staged:
        stage_sems = refs.pop()
    if placing:
        block_sem = refs.pop()
    if staged:
        (w_out, own), (w_other, other) = moves
        core = lax.rem(lax.axis_index("tp"), 2)
        moves = [pltpu.make_async_copy(w_other, other, stage_sems.at[SIDE])]
        for y in range(SIDE):
            here = pl.ds(pl.multiple_of((2 * y + core) * COLS, COLS), COLS)
            moves.append(pltpu.make_async_copy(w_out.at[:, here], own.at[y], stage_sems.at[y]))
    for move in moves:
        move.start()
    if final:
        keys, values, acc, maxima, sems = refs
    else:
        keys, values, sems = refs
        acc, maxima = outs
    count_rows = queries.shape[0]
    section = lax.axis_index("section")
    x, z = section // SIDE, section % SIDE
    count = jnp.int32(0)
    jobs = []
    for piece, offsets in zip(pieces, plan):
        for j, (dx, dz) in enumerate(offsets):
            source = lax.rem(x + dx, SIDE) * SIDE + lax.rem(z + dz, SIDE)
            needed = source < section
            here = pl.ds(j * HALF, HALF)
            there = pl.ds(pl.multiple_of(count * HALF, HALF), HALF)
            n = len(jobs)
            copies = (
                pltpu.make_async_copy(piece.at[here, :HD], keys.at[there, :], sems.at[n, 0]),
                pltpu.make_async_copy(piece.at[here, HD:], values.at[there, :HD], sems.at[n, 1]),
            )

            @pl.when(needed)
            def _():
                copies[0].start()
                copies[1].start()

            jobs.append((needed, copies))
            count = count + needed.astype(jnp.int32)
    if placing:
        cache[...] = jnp.zeros_like(cache) if diagonal else before[0][...]
        placed = jnp.int32(0)
        sources = [(piece, j * HALF, dx, dz, half)
                   for piece, offsets, half in zip(pieces, plan, halves)
                   for j, (dx, dz) in enumerate(offsets)]
        if diagonal:
            sources += [(begin[0], 0, 0, 0, 0), (begin[1], 0, 0, 0, 1)]
        for piece, row, dx, dz, half in sources:
            source = lax.rem(x + dx, SIDE) * SIDE + lax.rem(z + dz, SIDE)
            for rank in range(PAIR):
                slot = source * PAIR + rank
                inside = table[slot] - half * (HALF // BLOCK)
                found = (inside >= 0) & (inside < HALF // BLOCK)

                @pl.when(found)
                def _():
                    at = pl.ds(pl.multiple_of(row + inside * BLOCK, BLOCK), BLOCK)
                    pltpu.make_async_copy(piece.at[at, :], cache.at[slot], block_sem).start()

                placed = placed + found.astype(jnp.int32)
    values[:, HD:] = jnp.ones((values.shape[0], HD), BF)
    if diagonal:
        last = -(-len(jobs) // 4) * 4 * HALF
        for half in range(2):
            rows = slice(last + half * HALF, last + (half + 1) * HALF)
            keys[rows, :] = begin[half][:, :HD]
            values[rows, :HD] = begin[half][:, HD:]
        for start in range(0, ROWS, TILE):
            shape = (TILE, start + TILE)
            mask = lax.broadcasted_iota(jnp.int32, shape, 1) <= start + lax.broadcasted_iota(jnp.int32, shape, 0)
            kd, vd = keys[last : last + start + TILE, :], values[last : last + start + TILE, :]
            for h in range(HEADS):
                rows = pl.ds((start // SHARE * HEADS + h) * SHARE + start % SHARE, TILE)
                attend(queries[rows, :], kd, vd, acc, maxima, rows, mask, True)
    else:
        acc[...] = begin[0][...]
        maxima[...] = begin[1][...]
    for needed, copies in jobs:
        @pl.when(needed)
        def _():
            copies[0].wait()
            copies[1].wait()

    def part(base, size):
        at = pl.ds(pl.multiple_of(base, HALF), size)
        kd, vd = keys[at, :], values[at, :]
        for start in range(0, count_rows, TILE):
            rows = pl.ds(start, TILE)
            attend(queries[rows, :], kd, vd, acc, maxima, rows)

    def whole(i, _):
        part(i * 4 * HALF, 4 * HALF)
        return 0

    steps = (count + 3) // 4
    for n in range(3):
        @pl.when(count + n < steps * 4)
        def _():
            at = pl.ds(pl.multiple_of((count + n) * HALF, HALF), HALF)
            keys[at, :] = keys[:HALF, :]
            values[at, :] = jnp.zeros((HALF, 2 * HD), BF)

    lax.fori_loop(0, steps, whole, 0)

    if final:
        for h in range(HEADS):
            rows = slice(h * SHARE, (h + 1) * SHARE)
            outs[0][:, h * HD : (h + 1) * HD] = (acc[rows, :HD] / acc[rows, HD:]).astype(BF)
    if placing:
        def block(i, _):
            pltpu.make_async_copy(cache.at[0], cache.at[0], block_sem).wait()
            return 0

        lax.fori_loop(0, placed, block, 0)
    for move in moves:
        move.wait()


def attention(queries, begin, pieces, plan, name, diagonal=False, share=None, table=None, cache=None, halves=None, staged=()):
    subs = sum(len(p) for p in plan)
    final = share is not None
    rows = HEADS * SHARE if final else QROWS
    size = -(-subs // 4) * 4 * HALF + (ROWS if diagonal else 0)
    state_shape = [jax.ShapeDtypeStruct((rows, 2 * HD), F32), jax.ShapeDtypeStruct((rows, HD), F32)]
    scratch = [pltpu.VMEM((size, HD), BF), pltpu.VMEM((size, 2 * HD), BF)]
    if final:
        scratch += [pltpu.VMEM(s.shape, s.dtype) for s in state_shape]
        out_shape = [jax.ShapeDtypeStruct((SHARE, HEADS * HD), BF)]
        at = lambda i: (share, 0)
        in_specs = [pl.BlockSpec((rows, HD), at), pl.BlockSpec((rows, 2 * HD), at), pl.BlockSpec((rows, HD), at)]
        grid = (1,)
        out_specs = [pl.BlockSpec((SHARE, HEADS * HD), lambda i: (0, 0))]
    else:
        out_shape = state_shape
        in_specs = [WHOLE] * 3
        grid = ()
        out_specs = [WHOLE] * 2
    in_specs = in_specs + [ANY] * len(pieces)
    args = [queries, *begin, *pieces]
    scratch.append(pltpu.SemaphoreType.DMA((subs, 2)))
    if table is not None:
        in_specs.append(pl.BlockSpec(memory_space=pltpu.SMEM))
        args.append(table)
        if cache is not None:
            in_specs.append(WHOLE)
            args.append(cache)
        out_shape = out_shape + [jax.ShapeDtypeStruct((SIDE * SIDE * PAIR, BLOCK, 2 * HD), BF)]
        out_specs = out_specs + [WHOLE]
        scratch.append(pltpu.SemaphoreType.DMA)
    if staged:
        in_specs += [ANY] * len(staged)
        args += staged
        out_shape = out_shape + [jax.ShapeDtypeStruct(staged[1].shape, BF)] * 2
        out_specs = out_specs + [WHOLE] * len(staged)
        scratch.append(pltpu.SemaphoreType.DMA((SIDE + 1,)))
    return pl.pallas_call(
        functools.partial(attend_kernel, plan, halves, diagonal, final, len(staged)),
        grid=grid,
        in_specs=in_specs,
        out_specs=out_specs,
        out_shape=out_shape,
        scratch_shapes=scratch,
        compiler_params=limit(20),
        cost_estimate=pl.CostEstimate(
            flops=8 * rows * size * HD, bytes_accessed=8 << 20, transcendentals=rows * size
        ),
        name=name,
    )(*args)


def join_kernel(*refs):
    n = (len(refs) - 2) // 2
    for ins, out in ((refs[:n], refs[-2]), (refs[n : 2 * n], refs[-1])):
        for j, piece in enumerate(ins):
            out[j * HALF : (j + 1) * HALF, :] = piece[...]


def join(first, second):
    out = jax.ShapeDtypeStruct((len(first) * HALF, 2 * HD), BF)
    return pl.pallas_call(
        join_kernel,
        in_specs=[WHOLE] * (len(first) + len(second)),
        out_specs=[WHOLE] * 2,
        out_shape=[out] * 2,
        compiler_params=limit(8),
        cost_estimate=pl.CostEstimate(flops=0, bytes_accessed=2 << 20, transcendentals=0),
        name="join",
    )(*first, *second)


def cache_table(placement, section):
    owners = placement.reshape(SIDE * SIDE, ROWS // BLOCK)
    mine = owners == section
    before = jnp.arange(ROWS // BLOCK)[:, None] < jnp.arange(ROWS // BLOCK)[None, :]
    ranks = jnp.sum((mine[:, :, None] & before[None]).astype(jnp.int32), axis=1)
    hit = mine[:, None, :] & (ranks[:, None, :] == jnp.arange(PAIR)[None, :, None])
    number = jnp.arange(ROWS // BLOCK, dtype=jnp.int32) + 1
    return (jnp.sum(jnp.where(hit, number[None, None, :], 0), axis=-1) - 1).reshape(-1)


MID = SHARE // 2
PROJECT_LIMIT = 14


def term(offset, own, other, w_own, w_other):
    y = lax.rem(lax.axis_index("tp") // 2 + offset, SIDE)
    product = jnp.dot(own[...], w_own[y], preferred_element_type=F32)
    return product + jnp.dot(other[...], w_other[y], preferred_element_type=F32)


def opposite_kernel(own, other, w_own, w_other, top, bottom):
    product = term(2, own, other, w_own, w_other)
    top[...] = product[:MID].astype(BF)
    bottom[...] = product[MID:].astype(BF)


def neighbour_kernel(own, other, w_own, w_other, from_below, from_above, up, down):
    product = term(1, own, other, w_own, w_other)
    up[:MID] = (product[:MID] + from_below[...].astype(F32)).astype(BF)
    up[MID:] = product[MID:].astype(BF)
    product = term(3, own, other, w_own, w_other)
    down[:MID] = product[:MID].astype(BF)
    down[MID:] = (product[MID:] + from_above[...].astype(F32)).astype(BF)


def home_kernel(share, own, other, w_own, w_other, residual, out):
    rows = slice(share * SHARE, (share + 1) * SHARE)
    out[...] = residual[rows, :].astype(F32) + term(0, own, other, w_own, w_other)


def project(kernel, targets, terms, extra, out, name):
    return pl.pallas_call(
        kernel,
        in_specs=[WHOLE] * (len(terms) + len(extra)),
        out_specs=[WHOLE] * len(out),
        out_shape=[jax.ShapeDtypeStruct(shape, dtype) for shape, dtype in out],
        compiler_params=limit(PROJECT_LIMIT),
        cost_estimate=pl.CostEstimate(
            flops=4 * SHARE * 512 * COLS * targets, bytes_accessed=4 << 20, transcendentals=0
        ),
        name=name,
    )(*terms, *extra)


def finish_kernel(base, from_below, from_above, *refs):
    refs[-1][...] = (base[...] + from_below[...].astype(F32) + from_above[...].astype(F32)).astype(BF)


def finish(base, from_below, from_above, done, share):
    return pl.pallas_call(
        finish_kernel,
        grid=(1,),
        in_specs=[WHOLE] * 3 + [ANY] * len(done),
        out_specs=pl.BlockSpec((SHARE, COLS), lambda i: (share, 0)),
        out_shape=jax.ShapeDtypeStruct((ROWS, COLS), BF),
        input_output_aliases={3: 0} if done else {},
        compiler_params=limit(8),
        cost_estimate=pl.CostEstimate(flops=4 * SHARE * COLS, bytes_accessed=3 << 20, transcendentals=0),
        name="finish",
    )(base, from_below, from_above, *done)


def from_section(value, dx, dz):
    pairs = []
    for x in range(SIDE):
        for z in range(SIDE):
            pairs.append((((x + dx) % SIDE) * SIDE + (z + dz) % SIDE, x * SIDE + z))
    return lax.ppermute(value, "section", pairs)


def from_tp(value, dy, dc):
    pairs = []
    for y in range(SIDE):
        for c in range(2):
            pairs.append((((y + dy) % SIDE) * 2 + (c ^ dc), y * 2 + c))
    return lax.ppermute(value, "tp", pairs)


RING = (1, 3, 2)
ORDER = (0,) + RING


def per_device(tokens, gain, q_weight, q_bias, kv_weight, kv_bias, out_weight, placement):
    section = lax.axis_index("section")
    small, large = tables()
    factors, first, second, residual, w_send = norm_kv(
        tokens, gain[None, :], kv_weight, kv_bias[None, :], small, large, out_weight
    )
    w_other = from_tp(w_send, 0, 1)
    row_first = [from_section(first, 0, k) for k in RING]
    row_second = [from_section(second, k, 0) for k in RING]
    factors, row_first[0] = lax.optimization_barrier((factors, row_first[0]))
    queries = query(tokens, factors, gain[None, :], q_weight, q_bias[None, :], small, large)
    row_first[1], w_other, queries = lax.optimization_barrier((row_first[1], w_other, queries))
    all_first, all_second = join([first, *row_first], [second, *row_second])
    far_first = [from_section(all_first, k, 0) for k in RING]
    far_second = [from_section(all_second, 0, k) for k in RING]
    near = [[(0, k)] for k in RING] + [[(k, 0)] for k in RING]
    table = cache_table(placement, section)
    *state, cache = attention(
        queries,
        (first, second),
        row_first + row_second,
        near,
        "attention_near",
        diagonal=True,
        table=table,
        halves=[0] * 3 + [1] * 3,
    )
    far = [[(k, j) for j in ORDER] for k in RING], [[(j, k) for j in ORDER] for k in RING]
    *state, cache = attention(
        queries,
        state,
        far_first[:2] + far_second[:2],
        far[0][:2] + far[1][:2],
        "attention_far",
        table=table,
        cache=cache,
        halves=[0] * 2 + [1] * 2,
    )
    pieces, plan = far_first[2:] + far_second[2:], far[0][2:] + far[1][2:]
    (early,) = attention(queries, state, pieces, plan, "attention_last", share=0)
    late, cache, w_own, w_other = attention(
        queries,
        state,
        pieces,
        plan,
        "attention_last",
        share=1,
        table=table,
        cache=cache,
        halves=[0, 1],
        staged=(out_weight, w_other),
    )
    mixed = []
    for share, own in enumerate((early, late)):
        terms = (own, from_tp(own, 0, 1), w_own, w_other)
        top, bottom = project(opposite_kernel, 1, terms, [], [((MID, COLS), BF)] * 2, "project_opposite")
        from_below, from_above = from_tp(top, 3, 0), from_tp(bottom, 1, 0)
        up, down = project(
            neighbour_kernel, 2, terms, [from_below, from_above], [((SHARE, COLS), BF)] * 2, "project_neighbours"
        )
        from_below, from_above = from_tp(up, 3, 0), from_tp(down, 1, 0)
        (base,) = project(
            functools.partial(home_kernel, share), 1, terms, [residual], [((SHARE, COLS), F32)], "project_home"
        )
        mixed = [finish(base, from_below, from_above, mixed, share)]
    return mixed[0], cache


def solution(mesh):
    placed = (
        P("section", None),
        P(),
        P(None, "tp"),
        P("tp"),
        P(None, "tp"),
        P("tp"),
        P("tp", None),
        P(),
    )
    return jax.shard_map(
        per_device,
        mesh=mesh,
        in_specs=placed,
        out_specs=(P("section", "tp"), P("section", None, "tp")),
        check_vma=False,
    )
```

profile of v0, /device:TPU:14, one launch (start us, length us, event | category | flops | bytes accessed | tf_op | source)
XLA Modules:
  0.0 134.6 jit_solution(11563410757232215029)
XLA Ops:
  0.6 12.7 %norm_kv.1 = (f32[512,128]{1,0:T(8,128)}, bf16[256,256]{1,0:T(8,128)(2,1)}, bf16[256,256]{1,0:T(8,128)(2,1)}, bf16[512,1024]{1,0:T(8,128)(2,1)}, bf16[4,512,1024]{2,1,0:T(8,128)(2,1)}) custom-call(bf16[512,8192]{1,0:T(8,128)(2,1)} %tokens.3, f32[1,8192]{1,0:T(1,128)} %bitcast.5, bf16[8192,256]{1,0:T(8,128)(2,1)} %weight.2, f32[1,256]{1,0:T(1,128)} %bitcast.8, ...), custom_call_target="tpu_custom_call" | custom-call | flops 2147483648 | bytes 20971520 | tf_op jit(solution)/shard_map/norm_kv/pallas_call | solution.py:136
  13.3 0.1 collective-permute-start.1
  13.4 2.0 %collective-permute-start = (bf16[256,256]{1,0:T(8,128)(2,1)}, bf16[256,256]{1,0:T(8,128)(2,1)S(1)}, u32[]{:S(2)}, u32[]{:S(2)}) collective-permute-start(bf16[256,256]{1,0:T(8,128)(2,1)} %get-tuple-element.32.refs_1_.refs_0_), channel_id=1, source_target_pairs={{24,0},{0,8},{8,16},{16,24},{56,32},{32,40},{40,48},{48,56},{88,64... | collective-permute-start | bytes 393224 | tf_op jit(solution)/shard_map/ppermute | solution.py:545
  15.4 2.2 %collective-permute-start.2 = (bf16[256,256]{1,0:T(8,128)(2,1)}, bf16[256,256]{1,0:T(8,128)(2,1)S(1)}, u32[]{:S(2)}, u32[]{:S(2)}) collective-permute-start(bf16[256,256]{1,0:T(8,128)(2,1)} %get-tuple-element.32.refs_1_.refs_0_), channel_id=1, source_target_pairs={{8,0},{16,8},{24,16},{0,24},{40,32},{48,40},{56,48},{32,56},{72,64... | collective-permute-start | bytes 393224 | tf_op jit(solution)/shard_map/ppermute | solution.py:545
  17.6 1.8 %collective-permute-start.3 = (bf16[256,256]{1,0:T(8,128)(2,1)}, bf16[256,256]{1,0:T(8,128)(2,1)S(1)}, u32[]{:S(2)}, u32[]{:S(2)}) collective-permute-start(bf16[256,256]{1,0:T(8,128)(2,1)} %get-tuple-element.32.refs_1_.refs_0_), channel_id=1, source_target_pairs={{16,0},{24,8},{0,16},{8,24},{48,32},{56,40},{32,48},{40,56},{80,64... | collective-permute-start | bytes 393224 | tf_op jit(solution)/shard_map/ppermute | solution.py:545
  19.4 0.8 collective-permute-start.4
  20.2 0.1 eq.32
  20.3 0.1 convert_reduce_fusion
  20.5 0.1 select_reduce_fusion
  20.6 3.4 %collective-permute-done.2.refs_3_.refs_1_ = bf16[256,256]{1,0:T(8,128)(2,1)S(1)} collective-permute-done((bf16[256,256]{1,0:T(8,128)(2,1)}, bf16[256,256]{1,0:T(8,128)(2,1)S(1)}, u32[]{:S(2)}, u32[]{:S(2)}) %collective-permute-start.2) | collective-permute-done | bytes 131104 | tf_op jit(solution)/shard_map/ppermute | solution.py:545
  24.0 0.5 collective-permute-start.5
  24.5 0.0 collective-permute-done.refs_4_.refs_2_
  24.5 2.4 %collective-permute-start.6 = (bf16[256,256]{1,0:T(8,128)(2,1)}, bf16[256,256]{1,0:T(8,128)(2,1)S(1)}, u32[]{:S(2)}, u32[]{:S(2)}) collective-permute-start(bf16[256,256]{1,0:T(8,128)(2,1)} %get-tuple-element.37.refs_2_.refs_4_), channel_id=1, source_target_pairs={{64,0},{72,8},{80,16},{88,24},{96,32},{104,40},{112,48},{120,56},{... | collective-permute-start | bytes 393224 | tf_op jit(solution)/shard_map/ppermute | solution.py:545
  26.9 9.8 %query.1.refs_0_ = bf16[2048,128]{1,0:T(8,128)(2,1)} custom-call(bf16[512,8192]{1,0:T(8,128)(2,1)} %tokens.3, f32[512,128]{1,0:T(8,128)} %get-tuple-element.35.factors, f32[1,8192]{1,0:T(1,128)} %bitcast.6, bf16[8192,512]{1,0:T(8,128)(2,1)} %weight.3, f32[1,512]{1,0:T(1,128)} %bitcast.7, f32[512,256]{1,0:T(8,128)} %constant.17.clone.small, ...), custom_call_target="tpu_custom_call" | custom-call | flops 4294967296 | bytes 16777216 | tf_op jit(solution)/shard_map/query/pallas_call | solution.py:217
  36.7 0.0 collective-permute-done.1.refs_8_
  36.7 0.0 collective-permute-done.3.refs_5_.refs_3_
  36.7 0.0 collective-permute-done.4.refs_6_.refs_5_
  36.8 0.0 collective-permute-done.5.refs_7_.refs_6_
  36.8 0.0 collective-permute-done.6.refs_8_.refs_7_
  36.8 0.1 join.1
  36.9 0.1 collective-permute-start.7
  37.0 3.2 %collective-permute-start.8 = (bf16[1024,256]{1,0:T(8,128)(2,1)S(1)}, bf16[1024,256]{1,0:T(8,128)(2,1)S(1)}, u32[]{:S(2)}, u32[]{:S(2)}) collective-permute-start(bf16[1024,256]{1,0:T(8,128)(2,1)S(1)} %get-tuple-element.42), channel_id=1, source_target_pairs={{96,0},{104,8},{112,16},{120,24},{0,32},{8,40},{16,48},{24,56},{32... | collective-permute-start | bytes 1572872 | tf_op jit(solution)/shard_map/ppermute | solution.py:545
  40.2 3.6 %collective-permute-start.9 = (bf16[1024,256]{1,0:T(8,128)(2,1)S(1)}, bf16[1024,256]{1,0:T(8,128)(2,1)}, u32[]{:S(2)}, u32[]{:S(2)}) collective-permute-start(bf16[1024,256]{1,0:T(8,128)(2,1)S(1)} %get-tuple-element.43), channel_id=1, source_target_pairs={{8,0},{16,8},{24,16},{0,24},{40,32},{48,40},{56,48},{32,56},{72,64... | collective-permute-start | bytes 1572872 | tf_op jit(solution)/shard_map/ppermute | solution.py:545
  43.7 0.0 collective-permute-start.10
  43.7 0.1 copy.13
  43.8 0.1 sub.7.refs_9_.refs_7_.refs_5_
  43.9 0.1 collective-permute-start.11
  44.0 1.0 copy-done.1
  45.1 6.8 %attention_near.1 = (f32[2048,256]{1,0:T(8,128)S(1)}, f32[2048,128]{1,0:T(8,128)S(1)}, bf16[64,16,256]{2,1,0:T(8,128)(2,1)S(1)}) custom-call(bf16[2048,128]{1,0:T(8,128)(2,1)S(1)} %copy-done.1, bf16[256,256]{1,0:T(8,128)(2,1)S(1)} %copy-done.3, bf16[256,256]{1,0:T(8,128)(2,1)S(1)} %copy-done.4, bf16[256,256]{1,0:T(8,128)(2,1)S(1)} %collective-permute-done.2.refs_3_.refs_1_, ...), custom_call_target="tpu_custom_call" | custom-call | flops 5368709120 | bytes 8388608 | tf_op jit(solution)/shard_map/attention_near/pallas_call | solution.py:433
  51.9 0.0 collective-permute-done.7.refs_3_
  51.9 4.6 %collective-permute-start.12 = (bf16[1024,256]{1,0:T(8,128)(2,1)S(1)}, bf16[1024,256]{1,0:T(8,128)(2,1)S(1)}, u32[]{:S(2)}, u32[]{:S(2)}) collective-permute-start(bf16[1024,256]{1,0:T(8,128)(2,1)S(1)} %get-tuple-element.43), channel_id=1, source_target_pairs={{16,0},{24,8},{0,16},{8,24},{48,32},{56,40},{32,48},{40,56},{80,64... | collective-permute-start | bytes 1572872 | tf_op jit(solution)/shard_map/ppermute | solution.py:545
  56.5 2.4 %collective-permute-done.8.refs_4_ = bf16[1024,256]{1,0:T(8,128)(2,1)S(1)} collective-permute-done((bf16[1024,256]{1,0:T(8,128)(2,1)S(1)}, bf16[1024,256]{1,0:T(8,128)(2,1)S(1)}, u32[]{:S(2)}, u32[]{:S(2)}) %collective-permute-start.8) | collective-permute-done | bytes 524320 | tf_op jit(solution)/shard_map/ppermute | solution.py:545
  58.9 0.0 collective-permute-done.9.refs_5_
  58.9 9.4 %collective-permute-done.10.refs_6_ = bf16[1024,256]{1,0:T(8,128)(2,1)} collective-permute-done((bf16[1024,256]{1,0:T(8,128)(2,1)S(1)}, bf16[1024,256]{1,0:T(8,128)(2,1)}, u32[]{:S(2)}, u32[]{:S(2)}) %collective-permute-start.10) | collective-permute-done | bytes 524320 | tf_op jit(solution)/shard_map/ppermute | solution.py:545
  68.3 15.1 %attention_far.1 = (f32[2048,256]{1,0:T(8,128)S(1)}, f32[2048,128]{1,0:T(8,128)S(1)}, bf16[64,16,256]{2,1,0:T(8,128)(2,1)S(1)}) custom-call(bf16[2048,128]{1,0:T(8,128)(2,1)S(1)} %copy-done.2, f32[2048,256]{1,0:T(8,128)S(1)} %get-tuple-element.40.refs_1_, f32[2048,128]{1,0:T(8,128)S(1)} %get-tuple-element.41.refs_2_, ...), custom_call_target="tpu_custom_call" | custom-call | flops 8589934592 | bytes 8388608 | tf_op jit(solution)/shard_map/attention_far/pallas_call | solution.py:433
  83.4 4.2 %attention_last.3.own = bf16[256,512]{1,0:T(8,128)(2,1)S(1)} custom-call(bf16[2048,128]{1,0:T(8,128)(2,1)S(1)} %copy-done.2, f32[2048,256]{1,0:T(8,128)S(1)} %get-tuple-element.45.refs_1_, f32[2048,128]{1,0:T(8,128)S(1)} %get-tuple-element.46.refs_2_, bf16[1024,256]{1,0:T(8,128)(2,1)S(1)} %collective-permute-done.11.refs_3_, ...), custom_call_target="tpu_custom_call" | custom-call | flops 2147483648 | bytes 8388608 | tf_op jit(solution)/shard_map/attention_last/pallas_call | solution.py:433
  87.6 0.1 collective-permute-start.18
  87.7 7.0 %attention_last.2 = (bf16[256,512]{1,0:T(8,128)(2,1)S(1)}, bf16[64,16,256]{2,1,0:T(8,128)(2,1)}, bf16[4,512,1024]{2,1,0:T(8,128)(2,1)S(1)}, bf16[4,512,1024]{2,1,0:T(8,128)(2,1)S(1)}) custom-call(bf16[2048,128]{1,0:T(8,128)(2,1)S(1)} %copy-done.2, f32[2048,256]{1,0:T(8,128)S(1)} %get-tuple-element.45.refs_1_, f32[2048,128]{1,0:T(8,128)S(1)} %get-tuple-element.46.refs_2_, ...), custom_call_target="tpu_custom_call" | custom-call | flops 2147483648 | bytes 8388608 | tf_op jit(solution)/shard_map/attention_last/pallas_call | solution.py:433
  94.7 0.5 collective-permute-start.13
  95.2 0.7 project_opposite.3
  96.0 1.6 %collective-permute-start.19 = (bf16[128,1024]{1,0:T(8,128)(2,1)S(1)}, bf16[128,1024]{1,0:T(8,128)(2,1)S(1)}, u32[]{:S(2)}, u32[]{:S(2)}) collective-permute-start(bf16[128,1024]{1,0:T(8,128)(2,1)S(1)} %get-tuple-element.57), channel_id=1, source_target_pairs={{6,0},{7,1},{0,2},{1,3},{2,4},{3,5},{4,6},{5,7},{14,8},{15,9},{8,1... | collective-permute-start | bytes 786440 | tf_op jit(solution)/shard_map/ppermute | solution.py:553
  97.6 0.4 collective-permute-start.20
  98.1 0.0 collective-permute-done.13.other
  98.1 0.7 project_opposite.2
  98.8 1.6 %collective-permute-start.14 = (bf16[128,1024]{1,0:T(8,128)(2,1)S(1)}, bf16[128,1024]{1,0:T(8,128)(2,1)S(1)}, u32[]{:S(2)}, u32[]{:S(2)}) collective-permute-start(bf16[128,1024]{1,0:T(8,128)(2,1)S(1)} %get-tuple-element.53), channel_id=1, source_target_pairs={{6,0},{7,1},{0,2},{1,3},{2,4},{3,5},{4,6},{5,7},{14,8},{15,9},{8,1... | collective-permute-start | bytes 786440 | tf_op jit(solution)/shard_map/ppermute | solution.py:553
  100.5 0.4 collective-permute-start.15
  100.9 4.3 %collective-permute-done.19.from_below = bf16[128,1024]{1,0:T(8,128)(2,1)S(1)} collective-permute-done((bf16[128,1024]{1,0:T(8,128)(2,1)S(1)}, bf16[128,1024]{1,0:T(8,128)(2,1)S(1)}, u32[]{:S(2)}, u32[]{:S(2)}) %collective-permute-start.19) | collective-permute-done | bytes 262176 | tf_op jit(solution)/shard_map/ppermute | solution.py:553
  105.2 1.6 %collective-permute-done.20.from_above = bf16[128,1024]{1,0:T(8,128)(2,1)S(1)} collective-permute-done((bf16[128,1024]{1,0:T(8,128)(2,1)S(1)}, bf16[128,1024]{1,0:T(8,128)(2,1)S(1)}, u32[]{:S(2)}, u32[]{:S(2)}) %collective-permute-start.20) | collective-permute-done | bytes 262176 | tf_op jit(solution)/shard_map/ppermute | solution.py:553
  106.8 1.3 project_neighbours.3
  108.1 1.4 %collective-permute-start.21 = (bf16[256,1024]{1,0:T(8,128)(2,1)S(1)}, bf16[256,1024]{1,0:T(8,128)(2,1)S(1)}, u32[]{:S(2)}, u32[]{:S(2)}) collective-permute-start(bf16[256,1024]{1,0:T(8,128)(2,1)S(1)} %get-tuple-element.59), channel_id=1, source_target_pairs={{6,0},{7,1},{0,2},{1,3},{2,4},{3,5},{4,6},{5,7},{14,8},{15,9},{8,1... | collective-permute-start | bytes 1572872 | tf_op jit(solution)/shard_map/ppermute | solution.py:553
  109.5 0.7 collective-permute-start.22
  110.2 0.6 collective-permute-done.14.from_below
  110.8 1.6 %collective-permute-done.15.from_above = bf16[128,1024]{1,0:T(8,128)(2,1)S(1)} collective-permute-done((bf16[128,1024]{1,0:T(8,128)(2,1)S(1)}, bf16[128,1024]{1,0:T(8,128)(2,1)S(1)}, u32[]{:S(2)}, u32[]{:S(2)}) %collective-permute-start.15) | collective-permute-done | bytes 262176 | tf_op jit(solution)/shard_map/ppermute | solution.py:553
  112.4 1.3 project_neighbours.2
  113.8 1.4 %collective-permute-start.16 = (bf16[256,1024]{1,0:T(8,128)(2,1)S(1)}, bf16[256,1024]{1,0:T(8,128)(2,1)S(1)}, u32[]{:S(2)}, u32[]{:S(2)}) collective-permute-start(bf16[256,1024]{1,0:T(8,128)(2,1)S(1)} %get-tuple-element.55), channel_id=1, source_target_pairs={{6,0},{7,1},{0,2},{1,3},{2,4},{3,5},{4,6},{5,7},{14,8},{15,9},{8,1... | collective-permute-start | bytes 1572872 | tf_op jit(solution)/shard_map/ppermute | solution.py:553
  115.1 0.7 collective-permute-start.17
  115.9 0.7 project_home.2.base
  116.6 0.7 project_home.3.base
  117.4 5.7 %collective-permute-done.21.from_below = bf16[256,1024]{1,0:T(8,128)(2,1)S(1)} collective-permute-done((bf16[256,1024]{1,0:T(8,128)(2,1)S(1)}, bf16[256,1024]{1,0:T(8,128)(2,1)S(1)}, u32[]{:S(2)}, u32[]{:S(2)}) %collective-permute-start.21) | collective-permute-done | bytes 524320 | tf_op jit(solution)/shard_map/ppermute | solution.py:553
  123.1 1.3 collective-permute-done.22.from_above
  124.4 0.9 finish.2.refs_0_
  125.3 7.1 %collective-permute-done.16.from_below = bf16[256,1024]{1,0:T(8,128)(2,1)S(1)} collective-permute-done((bf16[256,1024]{1,0:T(8,128)(2,1)S(1)}, bf16[256,1024]{1,0:T(8,128)(2,1)S(1)}, u32[]{:S(2)}, u32[]{:S(2)}) %collective-permute-start.16) | collective-permute-done | bytes 524320 | tf_op jit(solution)/shard_map/ppermute | solution.py:553
  132.4 1.3 collective-permute-done.17.from_above
  133.7 0.9 finish.3
  (23 shorter events, 0.1 us)
Async XLA Ops:
  0.6 19.6 %copy-start.5 = (s32[512,1]{0,1:T(1,128)S(1)}, s32[512,1]{0,1:T(1,128)}, u32[]{:S(2)}) copy-start(s32[512,1]{0,1:T(1,128)} %param.17) | copy-start | bytes 6148
  13.3 23.4 %collective-permute-start.1 = (bf16[4,512,1024]{2,1,0:T(8,128)(2,1)}, bf16[4,512,1024]{2,1,0:T(8,128)(2,1)}, u32[]{:S(2)}, u32[]{:S(2)}) collective-permute-start(bf16[4,512,1024]{2,1,0:T(8,128)(2,1)} %get-tuple-element.33), channel_id=1, source_target_pairs={{1,0},{0,1},{3,2},{2,3},{5,4},{4,5},{7,6},{6,7},{9,8},{8,9},{11,10... | collective-permute-start | bytes 12582920 | tf_op jit(solution)/shard_map/ppermute | solution.py:553
  13.4 11.1 %collective-permute-start = (bf16[256,256]{1,0:T(8,128)(2,1)}, bf16[256,256]{1,0:T(8,128)(2,1)S(1)}, u32[]{:S(2)}, u32[]{:S(2)}) collective-permute-start(bf16[256,256]{1,0:T(8,128)(2,1)} %get-tuple-element.32.refs_1_.refs_0_), channel_id=1, source_target_pairs={{24,0},{0,8},{8,16},{16,24},{56,32},{32,40},{40,48},{48,56},{88,64... | collective-permute-start | bytes 393224 | tf_op jit(solution)/shard_map/ppermute | solution.py:545
  15.4 8.6 %collective-permute-start.2 = (bf16[256,256]{1,0:T(8,128)(2,1)}, bf16[256,256]{1,0:T(8,128)(2,1)S(1)}, u32[]{:S(2)}, u32[]{:S(2)}) collective-permute-start(bf16[256,256]{1,0:T(8,128)(2,1)} %get-tuple-element.32.refs_1_.refs_0_), channel_id=1, source_target_pairs={{8,0},{16,8},{24,16},{0,24},{40,32},{48,40},{56,48},{32,56},{72,64... | collective-permute-start | bytes 393224 | tf_op jit(solution)/shard_map/ppermute | solution.py:545
  17.6 19.1 %collective-permute-start.3 = (bf16[256,256]{1,0:T(8,128)(2,1)}, bf16[256,256]{1,0:T(8,128)(2,1)S(1)}, u32[]{:S(2)}, u32[]{:S(2)}) collective-permute-start(bf16[256,256]{1,0:T(8,128)(2,1)} %get-tuple-element.32.refs_1_.refs_0_), channel_id=1, source_target_pairs={{16,0},{24,8},{0,16},{8,24},{48,32},{56,40},{32,48},{40,56},{80,64... | collective-permute-start | bytes 393224 | tf_op jit(solution)/shard_map/ppermute | solution.py:545
  19.4 17.4 %collective-permute-start.4 = (bf16[256,256]{1,0:T(8,128)(2,1)}, bf16[256,256]{1,0:T(8,128)(2,1)S(1)}, u32[]{:S(2)}, u32[]{:S(2)}) collective-permute-start(bf16[256,256]{1,0:T(8,128)(2,1)} %get-tuple-element.37.refs_2_.refs_4_), channel_id=1, source_target_pairs={{32,0},{40,8},{48,16},{56,24},{64,32},{72,40},{80,48},{88,56},{96,... | collective-permute-start | bytes 393224 | tf_op jit(solution)/shard_map/ppermute | solution.py:545
  24.0 12.7 %collective-permute-start.5 = (bf16[256,256]{1,0:T(8,128)(2,1)}, bf16[256,256]{1,0:T(8,128)(2,1)S(1)}, u32[]{:S(2)}, u32[]{:S(2)}) collective-permute-start(bf16[256,256]{1,0:T(8,128)(2,1)} %get-tuple-element.37.refs_2_.refs_4_), channel_id=1, source_target_pairs={{96,0},{104,8},{112,16},{120,24},{0,32},{8,40},{16,48},{24,56},{32... | collective-permute-start | bytes 393224 | tf_op jit(solution)/shard_map/ppermute | solution.py:545
  24.5 12.3 %collective-permute-start.6 = (bf16[256,256]{1,0:T(8,128)(2,1)}, bf16[256,256]{1,0:T(8,128)(2,1)S(1)}, u32[]{:S(2)}, u32[]{:S(2)}) collective-permute-start(bf16[256,256]{1,0:T(8,128)(2,1)} %get-tuple-element.37.refs_2_.refs_4_), channel_id=1, source_target_pairs={{64,0},{72,8},{80,16},{88,24},{96,32},{104,40},{112,48},{120,56},{... | collective-permute-start | bytes 393224 | tf_op jit(solution)/shard_map/ppermute | solution.py:545
  26.9 9.9 %copy-start.3 = (bf16[256,256]{1,0:T(8,128)(2,1)S(1)}, bf16[256,256]{1,0:T(8,128)(2,1)}, u32[]{:S(2)}) copy-start(bf16[256,256]{1,0:T(8,128)(2,1)} %get-tuple-element.32.refs_1_.refs_0_) | copy-start | bytes 393220
  26.9 9.9 %copy-start.4 = (bf16[256,256]{1,0:T(8,128)(2,1)S(1)}, bf16[256,256]{1,0:T(8,128)(2,1)}, u32[]{:S(2)}) copy-start(bf16[256,256]{1,0:T(8,128)(2,1)} %get-tuple-element.37.refs_2_.refs_4_) | copy-start | bytes 393220
  36.9 15.0 %collective-permute-start.7 = (bf16[1024,256]{1,0:T(8,128)(2,1)S(1)}, bf16[1024,256]{1,0:T(8,128)(2,1)S(1)}, u32[]{:S(2)}, u32[]{:S(2)}) collective-permute-start(bf16[1024,256]{1,0:T(8,128)(2,1)S(1)} %get-tuple-element.42), channel_id=1, source_target_pairs={{32,0},{40,8},{48,16},{56,24},{64,32},{72,40},{80,48},{88,56},{96,... | collective-permute-start | bytes 1572872 | tf_op jit(solution)/shard_map/ppermute | solution.py:545
  37.0 21.9 %collective-permute-start.8 = (bf16[1024,256]{1,0:T(8,128)(2,1)S(1)}, bf16[1024,256]{1,0:T(8,128)(2,1)S(1)}, u32[]{:S(2)}, u32[]{:S(2)}) collective-permute-start(bf16[1024,256]{1,0:T(8,128)(2,1)S(1)} %get-tuple-element.42), channel_id=1, source_target_pairs={{96,0},{104,8},{112,16},{120,24},{0,32},{8,40},{16,48},{24,56},{32... | collective-permute-start | bytes 1572872 | tf_op jit(solution)/shard_map/ppermute | solution.py:545
  40.2 18.7 %collective-permute-start.9 = (bf16[1024,256]{1,0:T(8,128)(2,1)S(1)}, bf16[1024,256]{1,0:T(8,128)(2,1)}, u32[]{:S(2)}, u32[]{:S(2)}) collective-permute-start(bf16[1024,256]{1,0:T(8,128)(2,1)S(1)} %get-tuple-element.43), channel_id=1, source_target_pairs={{8,0},{16,8},{24,16},{0,24},{40,32},{48,40},{56,48},{32,56},{72,64... | collective-permute-start | bytes 1572872 | tf_op jit(solution)/shard_map/ppermute | solution.py:545
  43.7 24.5 %collective-permute-start.10 = (bf16[1024,256]{1,0:T(8,128)(2,1)S(1)}, bf16[1024,256]{1,0:T(8,128)(2,1)}, u32[]{:S(2)}, u32[]{:S(2)}) collective-permute-start(bf16[1024,256]{1,0:T(8,128)(2,1)S(1)} %get-tuple-element.43), channel_id=1, source_target_pairs={{24,0},{0,8},{8,16},{16,24},{56,32},{32,40},{40,48},{48,56},{88,64... | collective-permute-start | bytes 1572872 | tf_op jit(solution)/shard_map/ppermute | solution.py:545
  43.9 39.4 %collective-permute-start.11 = (bf16[1024,256]{1,0:T(8,128)(2,1)S(1)}, bf16[1024,256]{1,0:T(8,128)(2,1)S(1)}, u32[]{:S(2)}, u32[]{:S(2)}) collective-permute-start(bf16[1024,256]{1,0:T(8,128)(2,1)S(1)} %get-tuple-element.42), channel_id=1, source_target_pairs={{64,0},{72,8},{80,16},{88,24},{96,32},{104,40},{112,48},{120,56},{... | collective-permute-start | bytes 1572872 | tf_op jit(solution)/shard_map/ppermute | solution.py:545
  44.0 1.0 copy-start.1
  45.1 23.2 %copy-start.2 = (bf16[2048,128]{1,0:T(8,128)(2,1)S(1)}, bf16[2048,128]{1,0:T(8,128)(2,1)}, u32[]{:S(2)}) copy-start(bf16[2048,128]{1,0:T(8,128)(2,1)} %query.1.refs_0_) | copy-start | bytes 1572868
  51.9 31.5 %collective-permute-start.12 = (bf16[1024,256]{1,0:T(8,128)(2,1)S(1)}, bf16[1024,256]{1,0:T(8,128)(2,1)S(1)}, u32[]{:S(2)}, u32[]{:S(2)}) collective-permute-start(bf16[1024,256]{1,0:T(8,128)(2,1)S(1)} %get-tuple-element.43), channel_id=1, source_target_pairs={{16,0},{24,8},{0,16},{8,24},{48,32},{56,40},{32,48},{40,56},{80,64... | collective-permute-start | bytes 1572872 | tf_op jit(solution)/shard_map/ppermute | solution.py:545
  68.3 19.4 %slice-start = ((s8[8388608]{0:T(1024)(128)(4,1)}), s8[4194304]{0:T(1024)(128)(4,1)S(1)}, s32[]{:S(2)}) async-start(s8[8388608]{0:T(1024)(128)(4,1)} %bitcast.3), calls=%async_computation | async-start | bytes 8388608
  68.3 19.4 %slice-start.1 = ((s8[8388608]{0:T(1024)(128)(4,1)}), s8[4194304]{0:T(1024)(128)(4,1)S(1)}, s32[]{:S(2)}) async-start(s8[8388608]{0:T(1024)(128)(4,1)} %bitcast.3), calls=%async_computation.1 | async-start | bytes 8388608
  87.6 7.7 %collective-permute-start.18 = (bf16[256,512]{1,0:T(8,128)(2,1)S(1)}, bf16[256,512]{1,0:T(8,128)(2,1)S(1)}, u32[]{:S(2)}, u32[]{:S(2)}) collective-permute-start(bf16[256,512]{1,0:T(8,128)(2,1)S(1)} %attention_last.3.own), channel_id=1, source_target_pairs={{1,0},{0,1},{3,2},{2,3},{5,4},{4,5},{7,6},{6,7},{9,8},{8,9},{11,10... | collective-permute-start | bytes 786440 | tf_op jit(solution)/shard_map/ppermute | solution.py:553
  94.7 3.4 %collective-permute-start.13 = (bf16[256,512]{1,0:T(8,128)(2,1)S(1)}, bf16[256,512]{1,0:T(8,128)(2,1)S(1)}, u32[]{:S(2)}, u32[]{:S(2)}) collective-permute-start(bf16[256,512]{1,0:T(8,128)(2,1)S(1)} %get-tuple-element.49.own), channel_id=1, source_target_pairs={{1,0},{0,1},{3,2},{2,3},{5,4},{4,5},{7,6},{6,7},{9,8},{8,9},{11,10... | collective-permute-start | bytes 786440 | tf_op jit(solution)/shard_map/ppermute | solution.py:553
  96.0 9.2 %collective-permute-start.19 = (bf16[128,1024]{1,0:T(8,128)(2,1)S(1)}, bf16[128,1024]{1,0:T(8,128)(2,1)S(1)}, u32[]{:S(2)}, u32[]{:S(2)}) collective-permute-start(bf16[128,1024]{1,0:T(8,128)(2,1)S(1)} %get-tuple-element.57), channel_id=1, source_target_pairs={{6,0},{7,1},{0,2},{1,3},{2,4},{3,5},{4,6},{5,7},{14,8},{15,9},{8,1... | collective-permute-start | bytes 786440 | tf_op jit(solution)/shard_map/ppermute | solution.py:553
  97.6 9.2 %collective-permute-start.20 = (bf16[128,1024]{1,0:T(8,128)(2,1)S(1)}, bf16[128,1024]{1,0:T(8,128)(2,1)S(1)}, u32[]{:S(2)}, u32[]{:S(2)}) collective-permute-start(bf16[128,1024]{1,0:T(8,128)(2,1)S(1)} %get-tuple-element.58), channel_id=1, source_target_pairs={{2,0},{3,1},{4,2},{5,3},{6,4},{7,5},{0,6},{1,7},{10,8},{11,9},{12,... | collective-permute-start | bytes 786440 | tf_op jit(solution)/shard_map/ppermute | solution.py:553
  98.8 12.0 %collective-permute-start.14 = (bf16[128,1024]{1,0:T(8,128)(2,1)S(1)}, bf16[128,1024]{1,0:T(8,128)(2,1)S(1)}, u32[]{:S(2)}, u32[]{:S(2)}) collective-permute-start(bf16[128,1024]{1,0:T(8,128)(2,1)S(1)} %get-tuple-element.53), channel_id=1, source_target_pairs={{6,0},{7,1},{0,2},{1,3},{2,4},{3,5},{4,6},{5,7},{14,8},{15,9},{8,1... | collective-permute-start | bytes 786440 | tf_op jit(solution)/shard_map/ppermute | solution.py:553
  100.5 12.0 %collective-permute-start.15 = (bf16[128,1024]{1,0:T(8,128)(2,1)S(1)}, bf16[128,1024]{1,0:T(8,128)(2,1)S(1)}, u32[]{:S(2)}, u32[]{:S(2)}) collective-permute-start(bf16[128,1024]{1,0:T(8,128)(2,1)S(1)} %get-tuple-element.54), channel_id=1, source_target_pairs={{2,0},{3,1},{4,2},{5,3},{6,4},{7,5},{0,6},{1,7},{10,8},{11,9},{12,... | collective-permute-start | bytes 786440 | tf_op jit(solution)/shard_map/ppermute | solution.py:553
  108.1 14.9 %collective-permute-start.21 = (bf16[256,1024]{1,0:T(8,128)(2,1)S(1)}, bf16[256,1024]{1,0:T(8,128)(2,1)S(1)}, u32[]{:S(2)}, u32[]{:S(2)}) collective-permute-start(bf16[256,1024]{1,0:T(8,128)(2,1)S(1)} %get-tuple-element.59), channel_id=1, source_target_pairs={{6,0},{7,1},{0,2},{1,3},{2,4},{3,5},{4,6},{5,7},{14,8},{15,9},{8,1... | collective-permute-start | bytes 1572872 | tf_op jit(solution)/shard_map/ppermute | solution.py:553
  109.5 6.4 %copy-start = (bf16[512,1024]{1,0:T(8,128)(2,1)S(1)}, bf16[512,1024]{1,0:T(8,128)(2,1)}, u32[]{:S(2)}) copy-start(bf16[512,1024]{1,0:T(8,128)(2,1)} %get-tuple-element.52.residual) | copy-start | bytes 3145732
  109.5 14.9 %collective-permute-start.22 = (bf16[256,1024]{1,0:T(8,128)(2,1)S(1)}, bf16[256,1024]{1,0:T(8,128)(2,1)S(1)}, u32[]{:S(2)}, u32[]{:S(2)}) collective-permute-start(bf16[256,1024]{1,0:T(8,128)(2,1)S(1)} %get-tuple-element.60), channel_id=1, source_target_pairs={{2,0},{3,1},{4,2},{5,3},{6,4},{7,5},{0,6},{1,7},{10,8},{11,9},{12,... | collective-permute-start | bytes 1572872 | tf_op jit(solution)/shard_map/ppermute | solution.py:553
  113.8 18.6 %collective-permute-start.16 = (bf16[256,1024]{1,0:T(8,128)(2,1)S(1)}, bf16[256,1024]{1,0:T(8,128)(2,1)S(1)}, u32[]{:S(2)}, u32[]{:S(2)}) collective-permute-start(bf16[256,1024]{1,0:T(8,128)(2,1)S(1)} %get-tuple-element.55), channel_id=1, source_target_pairs={{6,0},{7,1},{0,2},{1,3},{2,4},{3,5},{4,6},{5,7},{14,8},{15,9},{8,1... | collective-permute-start | bytes 1572872 | tf_op jit(solution)/shard_map/ppermute | solution.py:553
  115.1 18.6 %collective-permute-start.17 = (bf16[256,1024]{1,0:T(8,128)(2,1)S(1)}, bf16[256,1024]{1,0:T(8,128)(2,1)S(1)}, u32[]{:S(2)}, u32[]{:S(2)}) collective-permute-start(bf16[256,1024]{1,0:T(8,128)(2,1)S(1)} %get-tuple-element.56), channel_id=1, source_target_pairs={{2,0},{3,1},{4,2},{5,3},{6,4},{7,5},{0,6},{1,7},{10,8},{11,9},{12,... | collective-permute-start | bytes 1572872 | tf_op jit(solution)/shard_map/ppermute | solution.py:553
where the time goes:
time: 135 us
  Pallas kernels  63 us (47%)
  waiting for transfers between devices  38.7 us (29%)
  starting transfers between devices  30.4 us (23%)
    pallas_call x4, Pallas kernels, attention(): pl.pallas_call(functools.partial(attend_kernel, plan, halves, diagonal, f...  33 us
    ppermute x11, waiting for transfers between devices, from_tp(): return lax.ppermute(value, 'tp', pairs)  23.5 us
    ppermute x12, starting transfers between devices, from_section(): return lax.ppermute(value, 'section', pairs)  21.3 us
    ppermute x12, waiting for transfers between devices, from_section(): return lax.ppermute(value, 'section', pairs)  15.2 us
    pallas_call x1, Pallas kernels, norm_kv(): pl.pallas_call(norm_kv_kernel, in_specs=[ANY, WHOLE, ANY, WHOLE, WHOLE, W...  12.7 us
    pallas_call x1, Pallas kernels, query(): pl.pallas_call(query_kernel, in_specs=[ANY, WHOLE, WHOLE, ANY, WHOLE, WHO...  9.79 us
    ppermute x11, starting transfers between devices, from_tp(): return lax.ppermute(value, 'tp', pairs)  9.1 us
    pallas_call x6, Pallas kernels, project(): pl.pallas_call(kernel, in_specs=[WHOLE] * (len(terms) + len(extra)), out_...  5.57 us
  transfers between devices with their start and end apart: 23, of which 11 were waited for; matrix products, arithmetic and copies ran while one was open for 0% of the time, Pallas kernels for 34%

commit v1 on v0

--- a/solution.py
+++ b/solution.py
@@ -570,8 +570,8 @@
     queries = query(tokens, factors, gain[None, :], q_weight, q_bias[None, :], small, large)
     row_first[1], w_other, queries = lax.optimization_barrier((row_first[1], w_other, queries))
     all_first, all_second = join([first, *row_first], [second, *row_second])
-    far_first = [from_section(all_first, k, 0) for k in RING]
-    far_second = [from_section(all_second, 0, k) for k in RING]
+    far_first = [from_section(all_first, k, 0) for k in RING[:2]]
+    far_second = [from_section(all_second, 0, k) for k in RING[:2]]
     near = [[(0, k)] for k in RING] + [[(k, 0)] for k in RING]
     table = cache_table(placement, section)
     *state, cache = attention(
@@ -584,8 +584,11 @@
         table=table,
         halves=[0] * 3 + [1] * 3,
     )
+    all_first, all_second, *state = lax.optimization_barrier((all_first, all_second, *state))
+    far_first.append(from_section(all_first, RING[2], 0))
+    far_second.append(from_section(all_second, 0, RING[2]))
     far = [[(k, j) for j in ORDER] for k in RING], [[(j, k) for j in ORDER] for k in RING]
-    *state, cache = attention(
+    *state, cache, w_own, w_other = attention(
         queries,
         state,
         far_first[:2] + far_second[:2],
@@ -594,10 +597,11 @@
         table=table,
         cache=cache,
         halves=[0] * 2 + [1] * 2,
+        staged=(out_weight, w_other),
     )
     pieces, plan = far_first[2:] + far_second[2:], far[0][2:] + far[1][2:]
     (early,) = attention(queries, state, pieces, plan, "attention_last", share=0)
-    late, cache, w_own, w_other = attention(
+    late, cache = attention(
         queries,
         state,
         pieces,
@@ -607,7 +611,6 @@
         table=table,
         cache=cache,
         halves=[0, 1],
-        staged=(out_weight, w_other),
     )
     mixed = []
     for share, own in enumerate((early, late)):

time: 135 us -> 134 us (level)
  local copies, waits for them, and re-layouts: 1.33 us -> 4.69 us
  starting transfers between devices: 30.4 us -> 27.9 us
  waiting for transfers between devices: 38.7 us -> 37.2 us
    unnamed x16 -> x14, local copies, waits for them, and re-layouts: 1.07 us -> 4.43 us
    ppermute x12, starting transfers between devices: 21.3 us -> 18.8 us  [from_section(): return lax.ppermute(value, 'section', pairs)]
    ppermute x12, waiting for transfers between devices: 15.2 us -> 13.6 us  [from_section(): return lax.ppermute(value, 'section', pairs)]
  transfers between devices with their start and end apart: 23 -> 23, of which waited for: 11 -> 10; matrix products, arithmetic and copies ran while one was open for 0% -> 0% of each run, Pallas kernels for 34% -> 33%
where the time goes in v1:
time: 134 us; the launch traced here: 133 us
  Pallas kernels  62.4 us (47%)
  waiting for transfers between devices  37.2 us (28%)
  starting transfers between devices  27.9 us (21%)
  local copies, waits for them, and re-layouts  4.69 us (4%)
    pallas_call x4, Pallas kernels, attention(): pl.pallas_call(functools.partial(attend_kernel, plan, halves, diagonal, f...  32.6 us
    ppermute x11, waiting for transfers between devices, from_tp(): return lax.ppermute(value, 'tp', pairs)  23.6 us
    ppermute x12, starting transfers between devices, from_section(): return lax.ppermute(value, 'section', pairs)  18.8 us
    ppermute x12, waiting for transfers between devices, from_section(): return lax.ppermute(value, 'section', pairs)  13.6 us
    pallas_call x1, Pallas kernels, norm_kv(): pl.pallas_call(norm_kv_kernel, in_specs=[ANY, WHOLE, ANY, WHOLE, WHOLE, W...  12.7 us
    pallas_call x1, Pallas kernels, query(): pl.pallas_call(query_kernel, in_specs=[ANY, WHOLE, WHOLE, ANY, WHOLE, WHO...  9.8 us
    ppermute x11, starting transfers between devices, from_tp(): return lax.ppermute(value, 'tp', pairs)  9.12 us
    pallas_call x6, Pallas kernels, project(): pl.pallas_call(kernel, in_specs=[WHOLE] * (len(terms) + len(extra)), out_...  5.42 us
  transfers between devices with their start and end apart: 23, of which 10 were waited for; matrix products, arithmetic and copies ran while one was open for 0% of the time, Pallas kernels for 33%

profile of v1, /device:TPU:14, one launch (start us, length us, event | category | flops | bytes accessed | tf_op | source)
XLA Modules:
  0.0 133.4 jit_solution(17617295525072718042)
XLA Ops:
  0.6 12.7 %norm_kv.1 = (f32[512,128]{1,0:T(8,128)}, bf16[256,256]{1,0:T(8,128)(2,1)}, bf16[256,256]{1,0:T(8,128)(2,1)}, bf16[512,1024]{1,0:T(8,128)(2,1)}, bf16[4,512,1024]{2,1,0:T(8,128)(2,1)}) custom-call(bf16[512,8192]{1,0:T(8,128)(2,1)} %tokens.3, f32[1,8192]{1,0:T(1,128)} %bitcast.3, bf16[8192,256]{1,0:T(8,128)(2,1)} %weight.2, f32[1,256]{1,0:T(1,128)} %bitcast.6, ...), custom_call_target="tpu_custom_call" | custom-call | flops 2147483648 | bytes 20971520 | tf_op jit(solution)/shard_map/norm_kv/pallas_call | solution.py:136
  13.3 0.1 collective-permute-start.1
  13.4 4.0 %collective-permute-start.3 = (bf16[256,256]{1,0:T(8,128)(2,1)}, bf16[256,256]{1,0:T(8,128)(2,1)S(1)}, u32[]{:S(2)}, u32[]{:S(2)}) collective-permute-start(bf16[256,256]{1,0:T(8,128)(2,1)} %get-tuple-element.36.refs_0_.refs_1_), channel_id=1, source_target_pairs={{16,0},{24,8},{0,16},{8,24},{48,32},{56,40},{32,48},{40,56},{80,64... | collective-permute-start | bytes 393224 | tf_op jit(solution)/shard_map/ppermute | solution.py:545
  17.4 0.7 collective-permute-start.2
  18.1 1.3 collective-permute-start
  19.4 1.4 %collective-permute-start.6 = (bf16[256,256]{1,0:T(8,128)(2,1)}, bf16[256,256]{1,0:T(8,128)(2,1)S(1)}, u32[]{:S(2)}, u32[]{:S(2)}) collective-permute-start(bf16[256,256]{1,0:T(8,128)(2,1)} %get-tuple-element.43.refs_4_.refs_2_), channel_id=1, source_target_pairs={{64,0},{72,8},{80,16},{88,24},{96,32},{104,40},{112,48},{120,56},{... | collective-permute-start | bytes 393224 | tf_op jit(solution)/shard_map/ppermute | solution.py:545
  20.8 0.1 eq.32
  20.9 0.1 convert_reduce_fusion
  21.1 0.1 select_reduce_fusion
  21.2 4.0 %collective-permute-done.2.refs_1_.refs_3_ = bf16[256,256]{1,0:T(8,128)(2,1)S(1)} collective-permute-done((bf16[256,256]{1,0:T(8,128)(2,1)}, bf16[256,256]{1,0:T(8,128)(2,1)S(1)}, u32[]{:S(2)}, u32[]{:S(2)}) %collective-permute-start.2) | collective-permute-done | bytes 131104 | tf_op jit(solution)/shard_map/ppermute | solution.py:545
  25.2 0.5 collective-permute-start.5
  25.7 0.0 collective-permute-done.refs_2_.refs_4_
  25.7 1.5 %collective-permute-start.4 = (bf16[256,256]{1,0:T(8,128)(2,1)}, bf16[256,256]{1,0:T(8,128)(2,1)S(1)}, u32[]{:S(2)}, u32[]{:S(2)}) collective-permute-start(bf16[256,256]{1,0:T(8,128)(2,1)} %get-tuple-element.43.refs_4_.refs_2_), channel_id=1, source_target_pairs={{32,0},{40,8},{48,16},{56,24},{64,32},{72,40},{80,48},{88,56},{96,... | collective-permute-start | bytes 393224 | tf_op jit(solution)/shard_map/ppermute | solution.py:545
  27.3 9.8 %query.1.refs_0_ = bf16[2048,128]{1,0:T(8,128)(2,1)} custom-call(bf16[512,8192]{1,0:T(8,128)(2,1)} %tokens.3, f32[512,128]{1,0:T(8,128)} %get-tuple-element.39.factors, f32[1,8192]{1,0:T(1,128)} %bitcast.4, bf16[8192,512]{1,0:T(8,128)(2,1)} %weight.3, f32[1,512]{1,0:T(1,128)} %bitcast.5, f32[512,256]{1,0:T(8,128)} %constant.17.clone.small, ...), custom_call_target="tpu_custom_call" | custom-call | flops 4294967296 | bytes 16777216 | tf_op jit(solution)/shard_map/query/pallas_call | solution.py:217
  37.1 0.0 collective-permute-done.1.refs_10_
  37.1 0.0 collective-permute-done.5.refs_6_.refs_7_
  37.2 0.1 join.1
  37.2 1.8 %collective-permute-start.8 = (bf16[1024,256]{1,0:T(8,128)(2,1)S(1)}, bf16[1024,256]{1,0:T(8,128)(2,1)S(1)}, u32[]{:S(2)}, u32[]{:S(2)}) collective-permute-start(bf16[1024,256]{1,0:T(8,128)(2,1)S(1)} %get-tuple-element.54), channel_id=1, source_target_pairs={{96,0},{104,8},{112,16},{120,24},{0,32},{8,40},{16,48},{24,56},{32... | collective-permute-start | bytes 1572872 | tf_op jit(solution)/shard_map/ppermute | solution.py:545
  39.0 0.3 collective-permute-start.7
  39.3 0.5 collective-permute-start.10
  39.9 2.7 %collective-permute-start.9 = (bf16[1024,256]{1,0:T(8,128)(2,1)S(1)}, bf16[1024,256]{1,0:T(8,128)(2,1)}, u32[]{:S(2)}, u32[]{:S(2)}) collective-permute-start(bf16[1024,256]{1,0:T(8,128)(2,1)S(1)} %get-tuple-element.55), channel_id=1, source_target_pairs={{8,0},{16,8},{24,16},{0,24},{40,32},{48,40},{56,48},{32,56},{72,64... | collective-permute-start | bytes 1572872 | tf_op jit(solution)/shard_map/ppermute | solution.py:545
  42.6 0.1 copy.13
  42.7 0.1 sub.7.refs_9_.refs_7_.refs_5_
  42.8 0.0 copy-start.2
  42.8 1.0 copy-done.2
  43.8 6.7 %attention_near.1 = (f32[2048,256]{1,0:T(8,128)S(1)}, f32[2048,128]{1,0:T(8,128)S(1)}, bf16[64,16,256]{2,1,0:T(8,128)(2,1)S(1)}) custom-call(bf16[2048,128]{1,0:T(8,128)(2,1)S(1)} %copy-done.2, bf16[256,256]{1,0:T(8,128)(2,1)S(1)} %copy-done.4, bf16[256,256]{1,0:T(8,128)(2,1)S(1)} %copy-done.5, bf16[256,256]{1,0:T(8,128)(2,1)S(1)} %collective-permute-done.2.refs_1_.refs_3_, ...), custom_call_target="tpu_custom_call" | custom-call | flops 5368709120 | bytes 8388608 | tf_op jit(solution)/shard_map/attention_near/pallas_call | solution.py:433
  50.5 1.4 %collective-permute-start.11 = (bf16[1024,256]{1,0:T(8,128)(2,1)S(1)}, bf16[1024,256]{1,0:T(8,128)(2,1)S(1)}, u32[]{:S(2)}, u32[]{:S(2)}) collective-permute-start(bf16[1024,256]{1,0:T(8,128)(2,1)S(1)} %get-tuple-element.54), channel_id=1, source_target_pairs={{64,0},{72,8},{80,16},{88,24},{96,32},{104,40},{112,48},{120,56},{... | collective-permute-start | bytes 1572872 | tf_op jit(solution)/shard_map/ppermute | solution.py:545
  51.9 0.0 collective-permute-done.8.refs_4_
  51.9 2.6 %collective-permute-start.12 = (bf16[1024,256]{1,0:T(8,128)(2,1)S(1)}, bf16[1024,256]{1,0:T(8,128)(2,1)S(1)}, u32[]{:S(2)}, u32[]{:S(2)}) collective-permute-start(bf16[1024,256]{1,0:T(8,128)(2,1)S(1)} %get-tuple-element.55), channel_id=1, source_target_pairs={{16,0},{24,8},{0,16},{8,24},{48,32},{56,40},{32,48},{40,56},{80,64... | collective-permute-start | bytes 1572872 | tf_op jit(solution)/shard_map/ppermute | solution.py:545
  54.5 9.5 %collective-permute-done.7.refs_3_ = bf16[1024,256]{1,0:T(8,128)(2,1)S(1)} collective-permute-done((bf16[1024,256]{1,0:T(8,128)(2,1)S(1)}, bf16[1024,256]{1,0:T(8,128)(2,1)S(1)}, u32[]{:S(2)}, u32[]{:S(2)}) %collective-permute-start.7) | collective-permute-done | bytes 524320 | tf_op jit(solution)/shard_map/ppermute | solution.py:545
  64.1 0.0 collective-permute-done.10.refs_6_
  64.1 0.0 copy-start
  64.1 3.4 %copy-done = bf16[512,8192]{1,0:T(8,128)(2,1)S(1)} copy-done((bf16[512,8192]{1,0:T(8,128)(2,1)S(1)}, bf16[512,8192]{1,0:T(8,128)(2,1)}, u32[]{:S(2)}) %copy-start) | copy-done | bytes 8388632
  67.5 15.6 %attention_far.1 = (f32[2048,256]{1,0:T(8,128)S(1)}, f32[2048,128]{1,0:T(8,128)S(1)}, bf16[64,16,256]{2,1,0:T(8,128)(2,1)S(1)}, bf16[4,512,1024]{2,1,0:T(8,128)(2,1)S(1)}, bf16[4,512,1024]{2,1,0:T(8,128)(2,1)S(1)}) custom-call(bf16[2048,128]{1,0:T(8,128)(2,1)S(1)} %copy-done.3, f32[2048,256]{1,0:T(8,128)S(1)} %get-tuple-element.48.refs_1_, ...), custom_call_target="tpu_custom_call" | custom-call | flops 8589934592 | bytes 8388608 | tf_op jit(solution)/shard_map/attention_far/pallas_call | solution.py:433
  83.1 0.0 collective-permute-done.11.refs_3_
  83.1 0.0 collective-permute-done.12.refs_4_
  83.1 4.1 %attention_last.3.own = bf16[256,512]{1,0:T(8,128)(2,1)S(1)} custom-call(bf16[2048,128]{1,0:T(8,128)(2,1)S(1)} %copy-done.3, f32[2048,256]{1,0:T(8,128)S(1)} %get-tuple-element.52.refs_1_, f32[2048,128]{1,0:T(8,128)S(1)} %get-tuple-element.53.refs_2_, bf16[1024,256]{1,0:T(8,128)(2,1)S(1)} %collective-permute-done.11.refs_3_, ...), custom_call_target="tpu_custom_call" | custom-call | flops 2147483648 | bytes 8388608 | tf_op jit(solution)/shard_map/attention_last/pallas_call | solution.py:433
  87.2 0.1 collective-permute-start.18
  87.3 6.2 %attention_last.2 = (bf16[256,512]{1,0:T(8,128)(2,1)S(1)}, bf16[64,16,256]{2,1,0:T(8,128)(2,1)}) custom-call(bf16[2048,128]{1,0:T(8,128)(2,1)S(1)} %copy-done.3, f32[2048,256]{1,0:T(8,128)S(1)} %get-tuple-element.52.refs_1_, f32[2048,128]{1,0:T(8,128)S(1)} %get-tuple-element.53.refs_2_, bf16[1024,256]{1,0:T(8,128)(2,1)S(1)} %collective-permute-done.11.refs_3_, ...), custom_call_target="tpu_custom_call" | custom-call | flops 2147483648 | bytes 8388608 | tf_op jit(solution)/shard_map/attention_last/pallas_call | solution.py:433
  93.5 0.6 collective-permute-start.13
  94.1 0.7 project_opposite.3
  94.8 1.6 %collective-permute-start.19 = (bf16[128,1024]{1,0:T(8,128)(2,1)S(1)}, bf16[128,1024]{1,0:T(8,128)(2,1)S(1)}, u32[]{:S(2)}, u32[]{:S(2)}) collective-permute-start(bf16[128,1024]{1,0:T(8,128)(2,1)S(1)} %get-tuple-element.65), channel_id=1, source_target_pairs={{6,0},{7,1},{0,2},{1,3},{2,4},{3,5},{4,6},{5,7},{14,8},{15,9},{8,1... | collective-permute-start | bytes 786440 | tf_op jit(solution)/shard_map/ppermute | solution.py:553
  96.4 0.4 collective-permute-start.20
  96.9 0.7 project_opposite.2
  97.6 1.6 %collective-permute-start.14 = (bf16[128,1024]{1,0:T(8,128)(2,1)S(1)}, bf16[128,1024]{1,0:T(8,128)(2,1)S(1)}, u32[]{:S(2)}, u32[]{:S(2)}) collective-permute-start(bf16[128,1024]{1,0:T(8,128)(2,1)S(1)} %get-tuple-element.61), channel_id=1, source_target_pairs={{6,0},{7,1},{0,2},{1,3},{2,4},{3,5},{4,6},{5,7},{14,8},{15,9},{8,1... | collective-permute-start | bytes 786440 | tf_op jit(solution)/shard_map/ppermute | solution.py:553
  99.3 0.4 collective-permute-start.15
  99.7 4.3 %collective-permute-done.19.from_below = bf16[128,1024]{1,0:T(8,128)(2,1)S(1)} collective-permute-done((bf16[128,1024]{1,0:T(8,128)(2,1)S(1)}, bf16[128,1024]{1,0:T(8,128)(2,1)S(1)}, u32[]{:S(2)}, u32[]{:S(2)}) %collective-permute-start.19) | collective-permute-done | bytes 262176 | tf_op jit(solution)/shard_map/ppermute | solution.py:553
  104.0 1.6 %collective-permute-done.20.from_above = bf16[128,1024]{1,0:T(8,128)(2,1)S(1)} collective-permute-done((bf16[128,1024]{1,0:T(8,128)(2,1)S(1)}, bf16[128,1024]{1,0:T(8,128)(2,1)S(1)}, u32[]{:S(2)}, u32[]{:S(2)}) %collective-permute-start.20) | collective-permute-done | bytes 262176 | tf_op jit(solution)/shard_map/ppermute | solution.py:553
  105.7 1.3 project_neighbours.3
  106.9 1.4 %collective-permute-start.21 = (bf16[256,1024]{1,0:T(8,128)(2,1)S(1)}, bf16[256,1024]{1,0:T(8,128)(2,1)S(1)}, u32[]{:S(2)}, u32[]{:S(2)}) collective-permute-start(bf16[256,1024]{1,0:T(8,128)(2,1)S(1)} %get-tuple-element.67), channel_id=1, source_target_pairs={{6,0},{7,1},{0,2},{1,3},{2,4},{3,5},{4,6},{5,7},{14,8},{15,9},{8,1... | collective-permute-start | bytes 1572872 | tf_op jit(solution)/shard_map/ppermute | solution.py:553
  108.3 0.7 collective-permute-start.22
  109.0 0.6 collective-permute-done.14.from_below
  109.7 1.6 %collective-permute-done.15.from_above = bf16[128,1024]{1,0:T(8,128)(2,1)S(1)} collective-permute-done((bf16[128,1024]{1,0:T(8,128)(2,1)S(1)}, bf16[128,1024]{1,0:T(8,128)(2,1)S(1)}, u32[]{:S(2)}, u32[]{:S(2)}) %collective-permute-start.15) | collective-permute-done | bytes 262176 | tf_op jit(solution)/shard_map/ppermute | solution.py:553
  111.3 1.3 project_neighbours.2
  112.6 1.4 %collective-permute-start.16 = (bf16[256,1024]{1,0:T(8,128)(2,1)S(1)}, bf16[256,1024]{1,0:T(8,128)(2,1)S(1)}, u32[]{:S(2)}, u32[]{:S(2)}) collective-permute-start(bf16[256,1024]{1,0:T(8,128)(2,1)S(1)} %get-tuple-element.63), channel_id=1, source_target_pairs={{6,0},{7,1},{0,2},{1,3},{2,4},{3,5},{4,6},{5,7},{14,8},{15,9},{8,1... | collective-permute-start | bytes 1572872 | tf_op jit(solution)/shard_map/ppermute | solution.py:553
  113.9 0.7 collective-permute-start.17
  114.7 0.7 project_home.3.base
  115.4 0.7 project_home.2.base
  116.1 5.7 %collective-permute-done.21.from_below = bf16[256,1024]{1,0:T(8,128)(2,1)S(1)} collective-permute-done((bf16[256,1024]{1,0:T(8,128)(2,1)S(1)}, bf16[256,1024]{1,0:T(8,128)(2,1)S(1)}, u32[]{:S(2)}, u32[]{:S(2)}) %collective-permute-start.21) | collective-permute-done | bytes 524320 | tf_op jit(solution)/shard_map/ppermute | solution.py:553
  121.8 1.3 collective-permute-done.22.from_above
  123.1 0.9 finish.2.refs_0_
  124.1 7.1 %collective-permute-done.16.from_below = bf16[256,1024]{1,0:T(8,128)(2,1)S(1)} collective-permute-done((bf16[256,1024]{1,0:T(8,128)(2,1)S(1)}, bf16[256,1024]{1,0:T(8,128)(2,1)S(1)}, u32[]{:S(2)}, u32[]{:S(2)}) %collective-permute-start.16) | collective-permute-done | bytes 524320 | tf_op jit(solution)/shard_map/ppermute | solution.py:553
  131.2 1.3 collective-permute-done.17.from_above
  132.5 0.9 finish.3
  (20 shorter events, 0.1 us)
Async XLA Ops:
  0.6 20.2 %copy-start.6 = (s32[512,1]{0,1:T(1,128)S(1)}, s32[512,1]{0,1:T(1,128)}, u32[]{:S(2)}) copy-start(s32[512,1]{0,1:T(1,128)} %param.17) | copy-start | bytes 6148
  13.3 23.8 %collective-permute-start.1 = (bf16[4,512,1024]{2,1,0:T(8,128)(2,1)}, bf16[4,512,1024]{2,1,0:T(8,128)(2,1)}, u32[]{:S(2)}, u32[]{:S(2)}) collective-permute-start(bf16[4,512,1024]{2,1,0:T(8,128)(2,1)} %get-tuple-element.37), channel_id=1, source_target_pairs={{1,0},{0,1},{3,2},{2,3},{5,4},{4,5},{7,6},{6,7},{9,8},{8,9},{11,10... | collective-permute-start | bytes 12582920 | tf_op jit(solution)/shard_map/ppermute | solution.py:553
  13.4 23.7 %collective-permute-start.3 = (bf16[256,256]{1,0:T(8,128)(2,1)}, bf16[256,256]{1,0:T(8,128)(2,1)S(1)}, u32[]{:S(2)}, u32[]{:S(2)}) collective-permute-start(bf16[256,256]{1,0:T(8,128)(2,1)} %get-tuple-element.36.refs_0_.refs_1_), channel_id=1, source_target_pairs={{16,0},{24,8},{0,16},{8,24},{48,32},{56,40},{32,48},{40,56},{80,64... | collective-permute-start | bytes 393224 | tf_op jit(solution)/shard_map/ppermute | solution.py:545
  17.4 7.9 %collective-permute-start.2 = (bf16[256,256]{1,0:T(8,128)(2,1)}, bf16[256,256]{1,0:T(8,128)(2,1)S(1)}, u32[]{:S(2)}, u32[]{:S(2)}) collective-permute-start(bf16[256,256]{1,0:T(8,128)(2,1)} %get-tuple-element.36.refs_0_.refs_1_), channel_id=1, source_target_pairs={{8,0},{16,8},{24,16},{0,24},{40,32},{48,40},{56,48},{32,56},{72,64... | collective-permute-start | bytes 393224 | tf_op jit(solution)/shard_map/ppermute | solution.py:545
  18.1 7.7 %collective-permute-start = (bf16[256,256]{1,0:T(8,128)(2,1)}, bf16[256,256]{1,0:T(8,128)(2,1)S(1)}, u32[]{:S(2)}, u32[]{:S(2)}) collective-permute-start(bf16[256,256]{1,0:T(8,128)(2,1)} %get-tuple-element.36.refs_0_.refs_1_), channel_id=1, source_target_pairs={{24,0},{0,8},{8,16},{16,24},{56,32},{32,40},{40,48},{48,56},{88,64... | collective-permute-start | bytes 393224 | tf_op jit(solution)/shard_map/ppermute | solution.py:545
  19.4 17.7 %collective-permute-start.6 = (bf16[256,256]{1,0:T(8,128)(2,1)}, bf16[256,256]{1,0:T(8,128)(2,1)S(1)}, u32[]{:S(2)}, u32[]{:S(2)}) collective-permute-start(bf16[256,256]{1,0:T(8,128)(2,1)} %get-tuple-element.43.refs_4_.refs_2_), channel_id=1, source_target_pairs={{64,0},{72,8},{80,16},{88,24},{96,32},{104,40},{112,48},{120,56},{... | collective-permute-start | bytes 393224 | tf_op jit(solution)/shard_map/ppermute | solution.py:545
  25.2 11.9 %collective-permute-start.5 = (bf16[256,256]{1,0:T(8,128)(2,1)}, bf16[256,256]{1,0:T(8,128)(2,1)S(1)}, u32[]{:S(2)}, u32[]{:S(2)}) collective-permute-start(bf16[256,256]{1,0:T(8,128)(2,1)} %get-tuple-element.43.refs_4_.refs_2_), channel_id=1, source_target_pairs={{96,0},{104,8},{112,16},{120,24},{0,32},{8,40},{16,48},{24,56},{32... | collective-permute-start | bytes 393224 | tf_op jit(solution)/shard_map/ppermute | solution.py:545
  25.7 11.4 %collective-permute-start.4 = (bf16[256,256]{1,0:T(8,128)(2,1)}, bf16[256,256]{1,0:T(8,128)(2,1)S(1)}, u32[]{:S(2)}, u32[]{:S(2)}) collective-permute-start(bf16[256,256]{1,0:T(8,128)(2,1)} %get-tuple-element.43.refs_4_.refs_2_), channel_id=1, source_target_pairs={{32,0},{40,8},{48,16},{56,24},{64,32},{72,40},{80,48},{88,56},{96,... | collective-permute-start | bytes 393224 | tf_op jit(solution)/shard_map/ppermute | solution.py:545
  27.3 9.9 %copy-start.4 = (bf16[256,256]{1,0:T(8,128)(2,1)S(1)}, bf16[256,256]{1,0:T(8,128)(2,1)}, u32[]{:S(2)}) copy-start(bf16[256,256]{1,0:T(8,128)(2,1)} %get-tuple-element.36.refs_0_.refs_1_) | copy-start | bytes 393220
  27.3 9.9 %copy-start.5 = (bf16[256,256]{1,0:T(8,128)(2,1)S(1)}, bf16[256,256]{1,0:T(8,128)(2,1)}, u32[]{:S(2)}) copy-start(bf16[256,256]{1,0:T(8,128)(2,1)} %get-tuple-element.43.refs_4_.refs_2_) | copy-start | bytes 393220
  37.2 14.7 %collective-permute-start.8 = (bf16[1024,256]{1,0:T(8,128)(2,1)S(1)}, bf16[1024,256]{1,0:T(8,128)(2,1)S(1)}, u32[]{:S(2)}, u32[]{:S(2)}) collective-permute-start(bf16[1024,256]{1,0:T(8,128)(2,1)S(1)} %get-tuple-element.54), channel_id=1, source_target_pairs={{96,0},{104,8},{112,16},{120,24},{0,32},{8,40},{16,48},{24,56},{32... | collective-permute-start | bytes 1572872 | tf_op jit(solution)/shard_map/ppermute | solution.py:545
  39.0 25.1 %collective-permute-start.7 = (bf16[1024,256]{1,0:T(8,128)(2,1)S(1)}, bf16[1024,256]{1,0:T(8,128)(2,1)S(1)}, u32[]{:S(2)}, u32[]{:S(2)}) collective-permute-start(bf16[1024,256]{1,0:T(8,128)(2,1)S(1)} %get-tuple-element.54), channel_id=1, source_target_pairs={{32,0},{40,8},{48,16},{56,24},{64,32},{72,40},{80,48},{88,56},{96,... | collective-permute-start | bytes 1572872 | tf_op jit(solution)/shard_map/ppermute | solution.py:545
  39.3 24.7 %collective-permute-start.10 = (bf16[1024,256]{1,0:T(8,128)(2,1)S(1)}, bf16[1024,256]{1,0:T(8,128)(2,1)}, u32[]{:S(2)}, u32[]{:S(2)}) collective-permute-start(bf16[1024,256]{1,0:T(8,128)(2,1)S(1)} %get-tuple-element.55), channel_id=1, source_target_pairs={{24,0},{0,8},{8,16},{16,24},{56,32},{32,40},{40,48},{48,56},{88,64... | collective-permute-start | bytes 1572872 | tf_op jit(solution)/shard_map/ppermute | solution.py:545
  39.9 24.2 %collective-permute-start.9 = (bf16[1024,256]{1,0:T(8,128)(2,1)S(1)}, bf16[1024,256]{1,0:T(8,128)(2,1)}, u32[]{:S(2)}, u32[]{:S(2)}) collective-permute-start(bf16[1024,256]{1,0:T(8,128)(2,1)S(1)} %get-tuple-element.55), channel_id=1, source_target_pairs={{8,0},{16,8},{24,16},{0,24},{40,32},{48,40},{56,48},{32,56},{72,64... | collective-permute-start | bytes 1572872 | tf_op jit(solution)/shard_map/ppermute | solution.py:545
  42.8 1.0 copy-start.2
  43.8 20.3 %copy-start.3 = (bf16[2048,128]{1,0:T(8,128)(2,1)S(1)}, bf16[2048,128]{1,0:T(8,128)(2,1)}, u32[]{:S(2)}) copy-start(bf16[2048,128]{1,0:T(8,128)(2,1)} %query.1.refs_0_) | copy-start | bytes 1572868
  50.5 32.6 %collective-permute-start.11 = (bf16[1024,256]{1,0:T(8,128)(2,1)S(1)}, bf16[1024,256]{1,0:T(8,128)(2,1)S(1)}, u32[]{:S(2)}, u32[]{:S(2)}) collective-permute-start(bf16[1024,256]{1,0:T(8,128)(2,1)S(1)} %get-tuple-element.54), channel_id=1, source_target_pairs={{64,0},{72,8},{80,16},{88,24},{96,32},{104,40},{112,48},{120,56},{... | collective-permute-start | bytes 1572872 | tf_op jit(solution)/shard_map/ppermute | solution.py:545
  51.9 31.2 %collective-permute-start.12 = (bf16[1024,256]{1,0:T(8,128)(2,1)S(1)}, bf16[1024,256]{1,0:T(8,128)(2,1)S(1)}, u32[]{:S(2)}, u32[]{:S(2)}) collective-permute-start(bf16[1024,256]{1,0:T(8,128)(2,1)S(1)} %get-tuple-element.55), channel_id=1, source_target_pairs={{16,0},{24,8},{0,16},{8,24},{48,32},{56,40},{32,48},{40,56},{80,64... | collective-permute-start | bytes 1572872 | tf_op jit(solution)/shard_map/ppermute | solution.py:545
  64.1 3.4 %copy-start = (bf16[512,8192]{1,0:T(8,128)(2,1)S(1)}, bf16[512,8192]{1,0:T(8,128)(2,1)}, u32[]{:S(2)}) copy-start(bf16[512,8192]{1,0:T(8,128)(2,1)} %refs_9_.1) | copy-start | bytes 25165828
  87.2 6.8 %collective-permute-start.18 = (bf16[256,512]{1,0:T(8,128)(2,1)S(1)}, bf16[256,512]{1,0:T(8,128)(2,1)S(1)}, u32[]{:S(2)}, u32[]{:S(2)}) collective-permute-start(bf16[256,512]{1,0:T(8,128)(2,1)S(1)} %attention_last.3.own), channel_id=1, source_target_pairs={{1,0},{0,1},{3,2},{2,3},{5,4},{4,5},{7,6},{6,7},{9,8},{8,9},{11,10... | collective-permute-start | bytes 786440 | tf_op jit(solution)/shard_map/ppermute | solution.py:553
  93.5 3.4 %collective-permute-start.13 = (bf16[256,512]{1,0:T(8,128)(2,1)S(1)}, bf16[256,512]{1,0:T(8,128)(2,1)S(1)}, u32[]{:S(2)}, u32[]{:S(2)}) collective-permute-start(bf16[256,512]{1,0:T(8,128)(2,1)S(1)} %get-tuple-element.57.own), channel_id=1, source_target_pairs={{1,0},{0,1},{3,2},{2,3},{5,4},{4,5},{7,6},{6,7},{9,8},{8,9},{11,10... | collective-permute-start | bytes 786440 | tf_op jit(solution)/shard_map/ppermute | solution.py:553
  94.8 9.2 %collective-permute-start.19 = (bf16[128,1024]{1,0:T(8,128)(2,1)S(1)}, bf16[128,1024]{1,0:T(8,128)(2,1)S(1)}, u32[]{:S(2)}, u32[]{:S(2)}) collective-permute-start(bf16[128,1024]{1,0:T(8,128)(2,1)S(1)} %get-tuple-element.65), channel_id=1, source_target_pairs={{6,0},{7,1},{0,2},{1,3},{2,4},{3,5},{4,6},{5,7},{14,8},{15,9},{8,1... | collective-permute-start | bytes 786440 | tf_op jit(solution)/shard_map/ppermute | solution.py:553
  96.4 9.2 %collective-permute-start.20 = (bf16[128,1024]{1,0:T(8,128)(2,1)S(1)}, bf16[128,1024]{1,0:T(8,128)(2,1)S(1)}, u32[]{:S(2)}, u32[]{:S(2)}) collective-permute-start(bf16[128,1024]{1,0:T(8,128)(2,1)S(1)} %get-tuple-element.66), channel_id=1, source_target_pairs={{2,0},{3,1},{4,2},{5,3},{6,4},{7,5},{0,6},{1,7},{10,8},{11,9},{12,... | collective-permute-start | bytes 786440 | tf_op jit(solution)/shard_map/ppermute | solution.py:553
  97.6 12.0 %collective-permute-start.14 = (bf16[128,1024]{1,0:T(8,128)(2,1)S(1)}, bf16[128,1024]{1,0:T(8,128)(2,1)S(1)}, u32[]{:S(2)}, u32[]{:S(2)}) collective-permute-start(bf16[128,1024]{1,0:T(8,128)(2,1)S(1)} %get-tuple-element.61), channel_id=1, source_target_pairs={{6,0},{7,1},{0,2},{1,3},{2,4},{3,5},{4,6},{5,7},{14,8},{15,9},{8,1... | collective-permute-start | bytes 786440 | tf_op jit(solution)/shard_map/ppermute | solution.py:553
  99.3 12.0 %collective-permute-start.15 = (bf16[128,1024]{1,0:T(8,128)(2,1)S(1)}, bf16[128,1024]{1,0:T(8,128)(2,1)S(1)}, u32[]{:S(2)}, u32[]{:S(2)}) collective-permute-start(bf16[128,1024]{1,0:T(8,128)(2,1)S(1)} %get-tuple-element.62), channel_id=1, source_target_pairs={{2,0},{3,1},{4,2},{5,3},{6,4},{7,5},{0,6},{1,7},{10,8},{11,9},{12,... | collective-permute-start | bytes 786440 | tf_op jit(solution)/shard_map/ppermute | solution.py:553
  106.9 14.9 %collective-permute-start.21 = (bf16[256,1024]{1,0:T(8,128)(2,1)S(1)}, bf16[256,1024]{1,0:T(8,128)(2,1)S(1)}, u32[]{:S(2)}, u32[]{:S(2)}) collective-permute-start(bf16[256,1024]{1,0:T(8,128)(2,1)S(1)} %get-tuple-element.67), channel_id=1, source_target_pairs={{6,0},{7,1},{0,2},{1,3},{2,4},{3,5},{4,6},{5,7},{14,8},{15,9},{8,1... | collective-permute-start | bytes 1572872 | tf_op jit(solution)/shard_map/ppermute | solution.py:553
  108.3 6.4 %copy-start.1 = (bf16[512,1024]{1,0:T(8,128)(2,1)S(1)}, bf16[512,1024]{1,0:T(8,128)(2,1)}, u32[]{:S(2)}) copy-start(bf16[512,1024]{1,0:T(8,128)(2,1)} %get-tuple-element.60.residual) | copy-start | bytes 3145732
  108.3 14.9 %collective-permute-start.22 = (bf16[256,1024]{1,0:T(8,128)(2,1)S(1)}, bf16[256,1024]{1,0:T(8,128)(2,1)S(1)}, u32[]{:S(2)}, u32[]{:S(2)}) collective-permute-start(bf16[256,1024]{1,0:T(8,128)(2,1)S(1)} %get-tuple-element.68), channel_id=1, source_target_pairs={{2,0},{3,1},{4,2},{5,3},{6,4},{7,5},{0,6},{1,7},{10,8},{11,9},{12,... | collective-permute-start | bytes 1572872 | tf_op jit(solution)/shard_map/ppermute | solution.py:553
  112.6 18.6 %collective-permute-start.16 = (bf16[256,1024]{1,0:T(8,128)(2,1)S(1)}, bf16[256,1024]{1,0:T(8,128)(2,1)S(1)}, u32[]{:S(2)}, u32[]{:S(2)}) collective-permute-start(bf16[256,1024]{1,0:T(8,128)(2,1)S(1)} %get-tuple-element.63), channel_id=1, source_target_pairs={{6,0},{7,1},{0,2},{1,3},{2,4},{3,5},{4,6},{5,7},{14,8},{15,9},{8,1... | collective-permute-start | bytes 1572872 | tf_op jit(solution)/shard_map/ppermute | solution.py:553
  113.9 18.6 %collective-permute-start.17 = (bf16[256,1024]{1,0:T(8,128)(2,1)S(1)}, bf16[256,1024]{1,0:T(8,128)(2,1)S(1)}, u32[]{:S(2)}, u32[]{:S(2)}) collective-permute-start(bf16[256,1024]{1,0:T(8,128)(2,1)S(1)} %get-tuple-element.64), channel_id=1, source_target_pairs={{2,0},{3,1},{4,2},{5,3},{6,4},{7,5},{0,6},{1,7},{10,8},{11,9},{12,... | collective-permute-start | bytes 1572872 | tf_op jit(solution)/shard_map/ppermute | solution.py:553

commit v2 on v1

--- a/solution.py
+++ b/solution.py
@@ -588,7 +588,7 @@
     far_first.append(from_section(all_first, RING[2], 0))
     far_second.append(from_section(all_second, 0, RING[2]))
     far = [[(k, j) for j in ORDER] for k in RING], [[(j, k) for j in ORDER] for k in RING]
-    *state, cache, w_own, w_other = attention(
+    *state, cache = attention(
         queries,
         state,
         far_first[:2] + far_second[:2],
@@ -597,11 +597,10 @@
         table=table,
         cache=cache,
         halves=[0] * 2 + [1] * 2,
-        staged=(out_weight, w_other),
     )
     pieces, plan = far_first[2:] + far_second[2:], far[0][2:] + far[1][2:]
     (early,) = attention(queries, state, pieces, plan, "attention_last", share=0)
-    late, cache = attention(
+    late, cache, w_own, w_other = attention(
         queries,
         state,
         pieces,
@@ -611,6 +610,7 @@
         table=table,
         cache=cache,
         halves=[0, 1],
+        staged=(out_weight, w_other),
     )
     mixed = []
     for share, own in enumerate((early, late)):

time: 134 us -> 135 us (level)
  local copies, waits for them, and re-layouts: 4.69 us -> 1.33 us
  starting transfers between devices: 27.9 us -> 30.3 us
  waiting for transfers between devices: 37.2 us -> 38.7 us
    unnamed x14 -> x16, local copies, waits for them, and re-layouts: 4.43 us -> 1.06 us
    ppermute x12, starting transfers between devices: 18.8 us -> 21.2 us  [from_section(): return lax.ppermute(value, 'section', pairs)]
    ppermute x12, waiting for transfers between devices: 13.6 us -> 15.2 us  [from_section(): return lax.ppermute(value, 'section', pairs)]
  transfers between devices with their start and end apart: 23 -> 23, of which waited for: 10 -> 10; matrix products, arithmetic and copies ran while one was open for 0% -> 0% of each run, Pallas kernels for 33% -> 34%
where the time goes in v2:
time: 135 us
  Pallas kernels  63.4 us (47%)
  waiting for transfers between devices  38.7 us (29%)
  starting transfers between devices  30.3 us (22%)
    pallas_call x4, Pallas kernels, attention(): pl.pallas_call(functools.partial(attend_kernel, plan, halves, diagonal, f...  33.4 us
    ppermute x11, waiting for transfers between devices, from_tp(): return lax.ppermute(value, 'tp', pairs)  23.5 us
    ppermute x12, starting transfers between devices, from_section(): return lax.ppermute(value, 'section', pairs)  21.2 us
    ppermute x12, waiting for transfers between devices, from_section(): return lax.ppermute(value, 'section', pairs)  15.2 us
    pallas_call x1, Pallas kernels, norm_kv(): pl.pallas_call(norm_kv_kernel, in_specs=[ANY, WHOLE, ANY, WHOLE, WHOLE, W...  12.7 us
    pallas_call x1, Pallas kernels, query(): pl.pallas_call(query_kernel, in_specs=[ANY, WHOLE, WHOLE, ANY, WHOLE, WHO...  9.79 us
    ppermute x11, starting transfers between devices, from_tp(): return lax.ppermute(value, 'tp', pairs)  9.1 us
    pallas_call x6, Pallas kernels, project(): pl.pallas_call(kernel, in_specs=[WHOLE] * (len(terms) + len(extra)), out_...  5.57 us
  transfers between devices with their start and end apart: 23, of which 10 were waited for; matrix products, arithmetic and copies ran while one was open for 0% of the time, Pallas kernels for 34%

profile of v2, /device:TPU:14, one launch (start us, length us, event | category | flops | bytes accessed | tf_op | source)
XLA Modules:
  0.0 134.9 jit_solution(323719503988289330)
XLA Ops:
  0.6 12.7 %norm_kv.1 = (f32[512,128]{1,0:T(8,128)}, bf16[256,256]{1,0:T(8,128)(2,1)}, bf16[256,256]{1,0:T(8,128)(2,1)}, bf16[512,1024]{1,0:T(8,128)(2,1)}, bf16[4,512,1024]{2,1,0:T(8,128)(2,1)}) custom-call(bf16[512,8192]{1,0:T(8,128)(2,1)} %tokens.3, f32[1,8192]{1,0:T(1,128)} %bitcast.5, bf16[8192,256]{1,0:T(8,128)(2,1)} %weight.2, f32[1,256]{1,0:T(1,128)} %bitcast.8, ...), custom_call_target="tpu_custom_call" | custom-call | flops 2147483648 | bytes 20971520 | tf_op jit(solution)/shard_map/norm_kv/pallas_call | solution.py:136
  13.3 0.1 collective-permute-start.1
  13.4 2.0 %collective-permute-start = (bf16[256,256]{1,0:T(8,128)(2,1)}, bf16[256,256]{1,0:T(8,128)(2,1)S(1)}, u32[]{:S(2)}, u32[]{:S(2)}) collective-permute-start(bf16[256,256]{1,0:T(8,128)(2,1)} %get-tuple-element.36.refs_0_.refs_1_), channel_id=1, source_target_pairs={{24,0},{0,8},{8,16},{16,24},{56,32},{32,40},{40,48},{48,56},{88,64... | collective-permute-start | bytes 393224 | tf_op jit(solution)/shard_map/ppermute | solution.py:545
  15.4 2.2 %collective-permute-start.2 = (bf16[256,256]{1,0:T(8,128)(2,1)}, bf16[256,256]{1,0:T(8,128)(2,1)S(1)}, u32[]{:S(2)}, u32[]{:S(2)}) collective-permute-start(bf16[256,256]{1,0:T(8,128)(2,1)} %get-tuple-element.36.refs_0_.refs_1_), channel_id=1, source_target_pairs={{8,0},{16,8},{24,16},{0,24},{40,32},{48,40},{56,48},{32,56},{72,64... | collective-permute-start | bytes 393224 | tf_op jit(solution)/shard_map/ppermute | solution.py:545
  17.6 1.8 %collective-permute-start.3 = (bf16[256,256]{1,0:T(8,128)(2,1)}, bf16[256,256]{1,0:T(8,128)(2,1)S(1)}, u32[]{:S(2)}, u32[]{:S(2)}) collective-permute-start(bf16[256,256]{1,0:T(8,128)(2,1)} %get-tuple-element.36.refs_0_.refs_1_), channel_id=1, source_target_pairs={{16,0},{24,8},{0,16},{8,24},{48,32},{56,40},{32,48},{40,56},{80,64... | collective-permute-start | bytes 393224 | tf_op jit(solution)/shard_map/ppermute | solution.py:545
  19.4 0.8 collective-permute-start.4
  20.2 0.1 eq.32
  20.3 0.1 convert_reduce_fusion
  20.5 0.1 select_reduce_fusion
  20.6 3.4 %collective-permute-done.2.refs_1_.refs_3_ = bf16[256,256]{1,0:T(8,128)(2,1)S(1)} collective-permute-done((bf16[256,256]{1,0:T(8,128)(2,1)}, bf16[256,256]{1,0:T(8,128)(2,1)S(1)}, u32[]{:S(2)}, u32[]{:S(2)}) %collective-permute-start.2) | collective-permute-done | bytes 131104 | tf_op jit(solution)/shard_map/ppermute | solution.py:545
  24.0 0.5 collective-permute-start.5
  24.5 2.4 %collective-permute-start.6 = (bf16[256,256]{1,0:T(8,128)(2,1)}, bf16[256,256]{1,0:T(8,128)(2,1)S(1)}, u32[]{:S(2)}, u32[]{:S(2)}) collective-permute-start(bf16[256,256]{1,0:T(8,128)(2,1)} %get-tuple-element.43.refs_4_.refs_2_), channel_id=1, source_target_pairs={{64,0},{72,8},{80,16},{88,24},{96,32},{104,40},{112,48},{120,56},{... | collective-permute-start | bytes 393224 | tf_op jit(solution)/shard_map/ppermute | solution.py:545
  26.9 9.8 %query.1.refs_0_ = bf16[2048,128]{1,0:T(8,128)(2,1)} custom-call(bf16[512,8192]{1,0:T(8,128)(2,1)} %tokens.3, f32[512,128]{1,0:T(8,128)} %get-tuple-element.39.factors, f32[1,8192]{1,0:T(1,128)} %bitcast.6, bf16[8192,512]{1,0:T(8,128)(2,1)} %weight.3, f32[1,512]{1,0:T(1,128)} %bitcast.7, f32[512,256]{1,0:T(8,128)} %constant.17.clone.small, ...), custom_call_target="tpu_custom_call" | custom-call | flops 4294967296 | bytes 16777216 | tf_op jit(solution)/shard_map/query/pallas_call | solution.py:217
  36.7 0.0 collective-permute-done.3.refs_3_.refs_5_
  36.7 0.0 collective-permute-done.4.refs_5_.refs_6_
  36.8 0.0 collective-permute-done.6.refs_7_.refs_8_
  36.8 0.1 join.1
  36.9 0.1 collective-permute-start.7
  37.0 3.2 %collective-permute-start.8 = (bf16[1024,256]{1,0:T(8,128)(2,1)S(1)}, bf16[1024,256]{1,0:T(8,128)(2,1)S(1)}, u32[]{:S(2)}, u32[]{:S(2)}) collective-permute-start(bf16[1024,256]{1,0:T(8,128)(2,1)S(1)} %get-tuple-element.53), channel_id=1, source_target_pairs={{96,0},{104,8},{112,16},{120,24},{0,32},{8,40},{16,48},{24,56},{32... | collective-permute-start | bytes 1572872 | tf_op jit(solution)/shard_map/ppermute | solution.py:545
  40.2 3.6 %collective-permute-start.9 = (bf16[1024,256]{1,0:T(8,128)(2,1)S(1)}, bf16[1024,256]{1,0:T(8,128)(2,1)}, u32[]{:S(2)}, u32[]{:S(2)}) collective-permute-start(bf16[1024,256]{1,0:T(8,128)(2,1)S(1)} %get-tuple-element.54), channel_id=1, source_target_pairs={{8,0},{16,8},{24,16},{0,24},{40,32},{48,40},{56,48},{32,56},{72,64... | collective-permute-start | bytes 1572872 | tf_op jit(solution)/shard_map/ppermute | solution.py:545
  43.7 0.0 collective-permute-start.10
  43.7 0.1 copy.13
  43.8 0.1 sub.7.refs_9_.refs_7_.refs_5_
  43.9 0.0 copy-start.1
  43.9 1.0 copy-done.1
  45.0 6.9 %attention_near.1 = (f32[2048,256]{1,0:T(8,128)S(1)}, f32[2048,128]{1,0:T(8,128)S(1)}, bf16[64,16,256]{2,1,0:T(8,128)(2,1)S(1)}) custom-call(bf16[2048,128]{1,0:T(8,128)(2,1)S(1)} %copy-done.1, bf16[256,256]{1,0:T(8,128)(2,1)S(1)} %copy-done.3, bf16[256,256]{1,0:T(8,128)(2,1)S(1)} %copy-done.4, bf16[256,256]{1,0:T(8,128)(2,1)S(1)} %collective-permute-done.2.refs_1_.refs_3_, ...), custom_call_target="tpu_custom_call" | custom-call | flops 5368709120 | bytes 8388608 | tf_op jit(solution)/shard_map/attention_near/pallas_call | solution.py:433
  51.8 0.1 collective-permute-start.11
  51.9 0.0 collective-permute-done.7.refs_3_
  51.9 4.5 %collective-permute-start.12 = (bf16[1024,256]{1,0:T(8,128)(2,1)S(1)}, bf16[1024,256]{1,0:T(8,128)(2,1)S(1)}, u32[]{:S(2)}, u32[]{:S(2)}) collective-permute-start(bf16[1024,256]{1,0:T(8,128)(2,1)S(1)} %get-tuple-element.54), channel_id=1, source_target_pairs={{16,0},{24,8},{0,16},{8,24},{48,32},{56,40},{32,48},{40,56},{80,64... | collective-permute-start | bytes 1572872 | tf_op jit(solution)/shard_map/ppermute | solution.py:545
  56.5 0.0 collective-permute-done.8.refs_4_
  56.5 0.0 collective-permute-done.9.refs_5_
  56.5 11.8 %collective-permute-done.10.refs_6_ = bf16[1024,256]{1,0:T(8,128)(2,1)} collective-permute-done((bf16[1024,256]{1,0:T(8,128)(2,1)S(1)}, bf16[1024,256]{1,0:T(8,128)(2,1)}, u32[]{:S(2)}, u32[]{:S(2)}) %collective-permute-start.10) | collective-permute-done | bytes 524320 | tf_op jit(solution)/shard_map/ppermute | solution.py:545
  68.3 15.2 %attention_far.1 = (f32[2048,256]{1,0:T(8,128)S(1)}, f32[2048,128]{1,0:T(8,128)S(1)}, bf16[64,16,256]{2,1,0:T(8,128)(2,1)S(1)}) custom-call(bf16[2048,128]{1,0:T(8,128)(2,1)S(1)} %copy-done.2, f32[2048,256]{1,0:T(8,128)S(1)} %get-tuple-element.48.refs_1_, f32[2048,128]{1,0:T(8,128)S(1)} %get-tuple-element.49.refs_2_, ...), custom_call_target="tpu_custom_call" | custom-call | flops 8589934592 | bytes 8388608 | tf_op jit(solution)/shard_map/attention_far/pallas_call | solution.py:433
  83.4 0.0 collective-permute-done.11.refs_3_
  83.5 0.0 collective-permute-done.12.refs_4_
  83.5 4.2 %attention_last.3.own = bf16[256,512]{1,0:T(8,128)(2,1)S(1)} custom-call(bf16[2048,128]{1,0:T(8,128)(2,1)S(1)} %copy-done.2, f32[2048,256]{1,0:T(8,128)S(1)} %get-tuple-element.51.refs_1_, f32[2048,128]{1,0:T(8,128)S(1)} %get-tuple-element.52.refs_2_, bf16[1024,256]{1,0:T(8,128)(2,1)S(1)} %collective-permute-done.11.refs_3_, ...), custom_call_target="tpu_custom_call" | custom-call | flops 2147483648 | bytes 8388608 | tf_op jit(solution)/shard_map/attention_last/pallas_call | solution.py:433
  87.6 0.1 collective-permute-start.18
  87.8 7.2 %attention_last.2 = (bf16[256,512]{1,0:T(8,128)(2,1)S(1)}, bf16[64,16,256]{2,1,0:T(8,128)(2,1)}, bf16[4,512,1024]{2,1,0:T(8,128)(2,1)S(1)}, bf16[4,512,1024]{2,1,0:T(8,128)(2,1)S(1)}) custom-call(bf16[2048,128]{1,0:T(8,128)(2,1)S(1)} %copy-done.2, f32[2048,256]{1,0:T(8,128)S(1)} %get-tuple-element.51.refs_1_, f32[2048,128]{1,0:T(8,128)S(1)} %get-tuple-element.52.refs_2_, ...), custom_call_target="tpu_custom_call" | custom-call | flops 2147483648 | bytes 8388608 | tf_op jit(solution)/shard_map/attention_last/pallas_call | solution.py:433
  95.0 0.5 collective-permute-start.13
  95.5 0.0 collective-permute-done.18.other
  95.5 0.7 project_opposite.3
  96.3 1.6 %collective-permute-start.19 = (bf16[128,1024]{1,0:T(8,128)(2,1)S(1)}, bf16[128,1024]{1,0:T(8,128)(2,1)S(1)}, u32[]{:S(2)}, u32[]{:S(2)}) collective-permute-start(bf16[128,1024]{1,0:T(8,128)(2,1)S(1)} %get-tuple-element.65), channel_id=1, source_target_pairs={{6,0},{7,1},{0,2},{1,3},{2,4},{3,5},{4,6},{5,7},{14,8},{15,9},{8,1... | collective-permute-start | bytes 786440 | tf_op jit(solution)/shard_map/ppermute | solution.py:553
  97.9 0.4 collective-permute-start.20
  98.4 0.7 project_opposite.2
  99.1 1.6 %collective-permute-start.14 = (bf16[128,1024]{1,0:T(8,128)(2,1)S(1)}, bf16[128,1024]{1,0:T(8,128)(2,1)S(1)}, u32[]{:S(2)}, u32[]{:S(2)}) collective-permute-start(bf16[128,1024]{1,0:T(8,128)(2,1)S(1)} %get-tuple-element.61), channel_id=1, source_target_pairs={{6,0},{7,1},{0,2},{1,3},{2,4},{3,5},{4,6},{5,7},{14,8},{15,9},{8,1... | collective-permute-start | bytes 786440 | tf_op jit(solution)/shard_map/ppermute | solution.py:553
  100.7 0.4 collective-permute-start.15
  101.2 4.3 %collective-permute-done.19.from_below = bf16[128,1024]{1,0:T(8,128)(2,1)S(1)} collective-permute-done((bf16[128,1024]{1,0:T(8,128)(2,1)S(1)}, bf16[128,1024]{1,0:T(8,128)(2,1)S(1)}, u32[]{:S(2)}, u32[]{:S(2)}) %collective-permute-start.19) | collective-permute-done | bytes 262176 | tf_op jit(solution)/shard_map/ppermute | solution.py:553
  105.5 1.6 %collective-permute-done.20.from_above = bf16[128,1024]{1,0:T(8,128)(2,1)S(1)} collective-permute-done((bf16[128,1024]{1,0:T(8,128)(2,1)S(1)}, bf16[128,1024]{1,0:T(8,128)(2,1)S(1)}, u32[]{:S(2)}, u32[]{:S(2)}) %collective-permute-start.20) | collective-permute-done | bytes 262176 | tf_op jit(solution)/shard_map/ppermute | solution.py:553
  107.1 1.3 project_neighbours.3
  108.4 1.4 %collective-permute-start.21 = (bf16[256,1024]{1,0:T(8,128)(2,1)S(1)}, bf16[256,1024]{1,0:T(8,128)(2,1)S(1)}, u32[]{:S(2)}, u32[]{:S(2)}) collective-permute-start(bf16[256,1024]{1,0:T(8,128)(2,1)S(1)} %get-tuple-element.67), channel_id=1, source_target_pairs={{6,0},{7,1},{0,2},{1,3},{2,4},{3,5},{4,6},{5,7},{14,8},{15,9},{8,1... | collective-permute-start | bytes 1572872 | tf_op jit(solution)/shard_map/ppermute | solution.py:553
  109.8 0.7 collective-permute-start.22
  110.5 0.6 collective-permute-done.14.from_below
  111.1 1.6 %collective-permute-done.15.from_above = bf16[128,1024]{1,0:T(8,128)(2,1)S(1)} collective-permute-done((bf16[128,1024]{1,0:T(8,128)(2,1)S(1)}, bf16[128,1024]{1,0:T(8,128)(2,1)S(1)}, u32[]{:S(2)}, u32[]{:S(2)}) %collective-permute-start.15) | collective-permute-done | bytes 262176 | tf_op jit(solution)/shard_map/ppermute | solution.py:553
  112.7 1.3 project_neighbours.2
  114.0 1.4 %collective-permute-start.16 = (bf16[256,1024]{1,0:T(8,128)(2,1)S(1)}, bf16[256,1024]{1,0:T(8,128)(2,1)S(1)}, u32[]{:S(2)}, u32[]{:S(2)}) collective-permute-start(bf16[256,1024]{1,0:T(8,128)(2,1)S(1)} %get-tuple-element.63), channel_id=1, source_target_pairs={{6,0},{7,1},{0,2},{1,3},{2,4},{3,5},{4,6},{5,7},{14,8},{15,9},{8,1... | collective-permute-start | bytes 1572872 | tf_op jit(solution)/shard_map/ppermute | solution.py:553
  115.4 0.7 collective-permute-start.17
  116.1 0.7 project_home.2.base
  116.9 0.8 project_home.3.base
  117.6 5.7 %collective-permute-done.21.from_below = bf16[256,1024]{1,0:T(8,128)(2,1)S(1)} collective-permute-done((bf16[256,1024]{1,0:T(8,128)(2,1)S(1)}, bf16[256,1024]{1,0:T(8,128)(2,1)S(1)}, u32[]{:S(2)}, u32[]{:S(2)}) %collective-permute-start.21) | collective-permute-done | bytes 524320 | tf_op jit(solution)/shard_map/ppermute | solution.py:553
  123.4 1.3 collective-permute-done.22.from_above
  124.6 0.9 finish.2.refs_0_
  125.6 7.1 %collective-permute-done.16.from_below = bf16[256,1024]{1,0:T(8,128)(2,1)S(1)} collective-permute-done((bf16[256,1024]{1,0:T(8,128)(2,1)S(1)}, bf16[256,1024]{1,0:T(8,128)(2,1)S(1)}, u32[]{:S(2)}, u32[]{:S(2)}) %collective-permute-start.16) | collective-permute-done | bytes 524320 | tf_op jit(solution)/shard_map/ppermute | solution.py:553
  132.7 1.3 collective-permute-done.17.from_above
  134.0 0.9 finish.3
  (23 shorter events, 0.1 us)
Async XLA Ops:
  0.6 19.6 %copy-start.5 = (s32[512,1]{0,1:T(1,128)S(1)}, s32[512,1]{0,1:T(1,128)}, u32[]{:S(2)}) copy-start(s32[512,1]{0,1:T(1,128)} %param.17) | copy-start | bytes 6148
  13.3 23.4 %collective-permute-start.1 = (bf16[4,512,1024]{2,1,0:T(8,128)(2,1)}, bf16[4,512,1024]{2,1,0:T(8,128)(2,1)}, u32[]{:S(2)}, u32[]{:S(2)}) collective-permute-start(bf16[4,512,1024]{2,1,0:T(8,128)(2,1)} %get-tuple-element.37), channel_id=1, source_target_pairs={{1,0},{0,1},{3,2},{2,3},{5,4},{4,5},{7,6},{6,7},{9,8},{8,9},{11,10... | collective-permute-start | bytes 12582920 | tf_op jit(solution)/shard_map/ppermute | solution.py:553
  13.4 11.1 %collective-permute-start = (bf16[256,256]{1,0:T(8,128)(2,1)}, bf16[256,256]{1,0:T(8,128)(2,1)S(1)}, u32[]{:S(2)}, u32[]{:S(2)}) collective-permute-start(bf16[256,256]{1,0:T(8,128)(2,1)} %get-tuple-element.36.refs_0_.refs_1_), channel_id=1, source_target_pairs={{24,0},{0,8},{8,16},{16,24},{56,32},{32,40},{40,48},{48,56},{88,64... | collective-permute-start | bytes 393224 | tf_op jit(solution)/shard_map/ppermute | solution.py:545
  15.4 8.6 %collective-permute-start.2 = (bf16[256,256]{1,0:T(8,128)(2,1)}, bf16[256,256]{1,0:T(8,128)(2,1)S(1)}, u32[]{:S(2)}, u32[]{:S(2)}) collective-permute-start(bf16[256,256]{1,0:T(8,128)(2,1)} %get-tuple-element.36.refs_0_.refs_1_), channel_id=1, source_target_pairs={{8,0},{16,8},{24,16},{0,24},{40,32},{48,40},{56,48},{32,56},{72,64... | collective-permute-start | bytes 393224 | tf_op jit(solution)/shard_map/ppermute | solution.py:545
  17.6 19.1 %collective-permute-start.3 = (bf16[256,256]{1,0:T(8,128)(2,1)}, bf16[256,256]{1,0:T(8,128)(2,1)S(1)}, u32[]{:S(2)}, u32[]{:S(2)}) collective-permute-start(bf16[256,256]{1,0:T(8,128)(2,1)} %get-tuple-element.36.refs_0_.refs_1_), channel_id=1, source_target_pairs={{16,0},{24,8},{0,16},{8,24},{48,32},{56,40},{32,48},{40,56},{80,64... | collective-permute-start | bytes 393224 | tf_op jit(solution)/shard_map/ppermute | solution.py:545
  19.4 17.4 %collective-permute-start.4 = (bf16[256,256]{1,0:T(8,128)(2,1)}, bf16[256,256]{1,0:T(8,128)(2,1)S(1)}, u32[]{:S(2)}, u32[]{:S(2)}) collective-permute-start(bf16[256,256]{1,0:T(8,128)(2,1)} %get-tuple-element.43.refs_4_.refs_2_), channel_id=1, source_target_pairs={{32,0},{40,8},{48,16},{56,24},{64,32},{72,40},{80,48},{88,56},{96,... | collective-permute-start | bytes 393224 | tf_op jit(solution)/shard_map/ppermute | solution.py:545
  24.0 12.7 %collective-permute-start.5 = (bf16[256,256]{1,0:T(8,128)(2,1)}, bf16[256,256]{1,0:T(8,128)(2,1)S(1)}, u32[]{:S(2)}, u32[]{:S(2)}) collective-permute-start(bf16[256,256]{1,0:T(8,128)(2,1)} %get-tuple-element.43.refs_4_.refs_2_), channel_id=1, source_target_pairs={{96,0},{104,8},{112,16},{120,24},{0,32},{8,40},{16,48},{24,56},{32... | collective-permute-start | bytes 393224 | tf_op jit(solution)/shard_map/ppermute | solution.py:545
  24.5 12.3 %collective-permute-start.6 = (bf16[256,256]{1,0:T(8,128)(2,1)}, bf16[256,256]{1,0:T(8,128)(2,1)S(1)}, u32[]{:S(2)}, u32[]{:S(2)}) collective-permute-start(bf16[256,256]{1,0:T(8,128)(2,1)} %get-tuple-element.43.refs_4_.refs_2_), channel_id=1, source_target_pairs={{64,0},{72,8},{80,16},{88,24},{96,32},{104,40},{112,48},{120,56},{... | collective-permute-start | bytes 393224 | tf_op jit(solution)/shard_map/ppermute | solution.py:545
  26.9 9.9 %copy-start.3 = (bf16[256,256]{1,0:T(8,128)(2,1)S(1)}, bf16[256,256]{1,0:T(8,128)(2,1)}, u32[]{:S(2)}) copy-start(bf16[256,256]{1,0:T(8,128)(2,1)} %get-tuple-element.36.refs_0_.refs_1_) | copy-start | bytes 393220
  26.9 9.9 %copy-start.4 = (bf16[256,256]{1,0:T(8,128)(2,1)S(1)}, bf16[256,256]{1,0:T(8,128)(2,1)}, u32[]{:S(2)}) copy-start(bf16[256,256]{1,0:T(8,128)(2,1)} %get-tuple-element.43.refs_4_.refs_2_) | copy-start | bytes 393220
  36.9 15.1 %collective-permute-start.7 = (bf16[1024,256]{1,0:T(8,128)(2,1)S(1)}, bf16[1024,256]{1,0:T(8,128)(2,1)S(1)}, u32[]{:S(2)}, u32[]{:S(2)}) collective-permute-start(bf16[1024,256]{1,0:T(8,128)(2,1)S(1)} %get-tuple-element.53), channel_id=1, source_target_pairs={{32,0},{40,8},{48,16},{56,24},{64,32},{72,40},{80,48},{88,56},{96,... | collective-permute-start | bytes 1572872 | tf_op jit(solution)/shard_map/ppermute | solution.py:545
  37.0 19.5 %collective-permute-start.8 = (bf16[1024,256]{1,0:T(8,128)(2,1)S(1)}, bf16[1024,256]{1,0:T(8,128)(2,1)S(1)}, u32[]{:S(2)}, u32[]{:S(2)}) collective-permute-start(bf16[1024,256]{1,0:T(8,128)(2,1)S(1)} %get-tuple-element.53), channel_id=1, source_target_pairs={{96,0},{104,8},{112,16},{120,24},{0,32},{8,40},{16,48},{24,56},{32... | collective-permute-start | bytes 1572872 | tf_op jit(solution)/shard_map/ppermute | solution.py:545
  40.2 16.3 %collective-permute-start.9 = (bf16[1024,256]{1,0:T(8,128)(2,1)S(1)}, bf16[1024,256]{1,0:T(8,128)(2,1)}, u32[]{:S(2)}, u32[]{:S(2)}) collective-permute-start(bf16[1024,256]{1,0:T(8,128)(2,1)S(1)} %get-tuple-element.54), channel_id=1, source_target_pairs={{8,0},{16,8},{24,16},{0,24},{40,32},{48,40},{56,48},{32,56},{72,64... | collective-permute-start | bytes 1572872 | tf_op jit(solution)/shard_map/ppermute | solution.py:545
  43.7 24.5 %collective-permute-start.10 = (bf16[1024,256]{1,0:T(8,128)(2,1)S(1)}, bf16[1024,256]{1,0:T(8,128)(2,1)}, u32[]{:S(2)}, u32[]{:S(2)}) collective-permute-start(bf16[1024,256]{1,0:T(8,128)(2,1)S(1)} %get-tuple-element.54), channel_id=1, source_target_pairs={{24,0},{0,8},{8,16},{16,24},{56,32},{32,40},{40,48},{48,56},{88,64... | collective-permute-start | bytes 1572872 | tf_op jit(solution)/shard_map/ppermute | solution.py:545
  43.9 1.0 copy-start.1
  45.0 23.3 %copy-start.2 = (bf16[2048,128]{1,0:T(8,128)(2,1)S(1)}, bf16[2048,128]{1,0:T(8,128)(2,1)}, u32[]{:S(2)}) copy-start(bf16[2048,128]{1,0:T(8,128)(2,1)} %query.1.refs_0_) | copy-start | bytes 1572868
  51.8 31.6 %collective-permute-start.11 = (bf16[1024,256]{1,0:T(8,128)(2,1)S(1)}, bf16[1024,256]{1,0:T(8,128)(2,1)S(1)}, u32[]{:S(2)}, u32[]{:S(2)}) collective-permute-start(bf16[1024,256]{1,0:T(8,128)(2,1)S(1)} %get-tuple-element.53), channel_id=1, source_target_pairs={{64,0},{72,8},{80,16},{88,24},{96,32},{104,40},{112,48},{120,56},{... | collective-permute-start | bytes 1572872 | tf_op jit(solution)/shard_map/ppermute | solution.py:545
  51.9 31.5 %collective-permute-start.12 = (bf16[1024,256]{1,0:T(8,128)(2,1)S(1)}, bf16[1024,256]{1,0:T(8,128)(2,1)S(1)}, u32[]{:S(2)}, u32[]{:S(2)}) collective-permute-start(bf16[1024,256]{1,0:T(8,128)(2,1)S(1)} %get-tuple-element.54), channel_id=1, source_target_pairs={{16,0},{24,8},{0,16},{8,24},{48,32},{56,40},{32,48},{40,56},{80,64... | collective-permute-start | bytes 1572872 | tf_op jit(solution)/shard_map/ppermute | solution.py:545
  68.3 19.5 %slice-start = ((s8[8388608]{0:T(1024)(128)(4,1)}), s8[4194304]{0:T(1024)(128)(4,1)S(1)}, s32[]{:S(2)}) async-start(s8[8388608]{0:T(1024)(128)(4,1)} %bitcast.3), calls=%async_computation | async-start | bytes 8388608
  68.3 19.5 %slice-start.1 = ((s8[8388608]{0:T(1024)(128)(4,1)}), s8[4194304]{0:T(1024)(128)(4,1)S(1)}, s32[]{:S(2)}) async-start(s8[8388608]{0:T(1024)(128)(4,1)} %bitcast.3), calls=%async_computation.1 | async-start | bytes 8388608
  87.6 7.9 %collective-permute-start.18 = (bf16[256,512]{1,0:T(8,128)(2,1)S(1)}, bf16[256,512]{1,0:T(8,128)(2,1)S(1)}, u32[]{:S(2)}, u32[]{:S(2)}) collective-permute-start(bf16[256,512]{1,0:T(8,128)(2,1)S(1)} %attention_last.3.own), channel_id=1, source_target_pairs={{1,0},{0,1},{3,2},{2,3},{5,4},{4,5},{7,6},{6,7},{9,8},{8,9},{11,10... | collective-permute-start | bytes 786440 | tf_op jit(solution)/shard_map/ppermute | solution.py:553
  95.0 3.4 %collective-permute-start.13 = (bf16[256,512]{1,0:T(8,128)(2,1)S(1)}, bf16[256,512]{1,0:T(8,128)(2,1)S(1)}, u32[]{:S(2)}, u32[]{:S(2)}) collective-permute-start(bf16[256,512]{1,0:T(8,128)(2,1)S(1)} %get-tuple-element.57.own), channel_id=1, source_target_pairs={{1,0},{0,1},{3,2},{2,3},{5,4},{4,5},{7,6},{6,7},{9,8},{8,9},{11,10... | collective-permute-start | bytes 786440 | tf_op jit(solution)/shard_map/ppermute | solution.py:553
  96.3 9.2 %collective-permute-start.19 = (bf16[128,1024]{1,0:T(8,128)(2,1)S(1)}, bf16[128,1024]{1,0:T(8,128)(2,1)S(1)}, u32[]{:S(2)}, u32[]{:S(2)}) collective-permute-start(bf16[128,1024]{1,0:T(8,128)(2,1)S(1)} %get-tuple-element.65), channel_id=1, source_target_pairs={{6,0},{7,1},{0,2},{1,3},{2,4},{3,5},{4,6},{5,7},{14,8},{15,9},{8,1... | collective-permute-start | bytes 786440 | tf_op jit(solution)/shard_map/ppermute | solution.py:553
  97.9 9.2 %collective-permute-start.20 = (bf16[128,1024]{1,0:T(8,128)(2,1)S(1)}, bf16[128,1024]{1,0:T(8,128)(2,1)S(1)}, u32[]{:S(2)}, u32[]{:S(2)}) collective-permute-start(bf16[128,1024]{1,0:T(8,128)(2,1)S(1)} %get-tuple-element.66), channel_id=1, source_target_pairs={{2,0},{3,1},{4,2},{5,3},{6,4},{7,5},{0,6},{1,7},{10,8},{11,9},{12,... | collective-permute-start | bytes 786440 | tf_op jit(solution)/shard_map/ppermute | solution.py:553
  99.1 12.0 %collective-permute-start.14 = (bf16[128,1024]{1,0:T(8,128)(2,1)S(1)}, bf16[128,1024]{1,0:T(8,128)(2,1)S(1)}, u32[]{:S(2)}, u32[]{:S(2)}) collective-permute-start(bf16[128,1024]{1,0:T(8,128)(2,1)S(1)} %get-tuple-element.61), channel_id=1, source_target_pairs={{6,0},{7,1},{0,2},{1,3},{2,4},{3,5},{4,6},{5,7},{14,8},{15,9},{8,1... | collective-permute-start | bytes 786440 | tf_op jit(solution)/shard_map/ppermute | solution.py:553
  100.7 12.0 %collective-permute-start.15 = (bf16[128,1024]{1,0:T(8,128)(2,1)S(1)}, bf16[128,1024]{1,0:T(8,128)(2,1)S(1)}, u32[]{:S(2)}, u32[]{:S(2)}) collective-permute-start(bf16[128,1024]{1,0:T(8,128)(2,1)S(1)} %get-tuple-element.62), channel_id=1, source_target_pairs={{2,0},{3,1},{4,2},{5,3},{6,4},{7,5},{0,6},{1,7},{10,8},{11,9},{12,... | collective-permute-start | bytes 786440 | tf_op jit(solution)/shard_map/ppermute | solution.py:553
  108.4 14.9 %collective-permute-start.21 = (bf16[256,1024]{1,0:T(8,128)(2,1)S(1)}, bf16[256,1024]{1,0:T(8,128)(2,1)S(1)}, u32[]{:S(2)}, u32[]{:S(2)}) collective-permute-start(bf16[256,1024]{1,0:T(8,128)(2,1)S(1)} %get-tuple-element.67), channel_id=1, source_target_pairs={{6,0},{7,1},{0,2},{1,3},{2,4},{3,5},{4,6},{5,7},{14,8},{15,9},{8,1... | collective-permute-start | bytes 1572872 | tf_op jit(solution)/shard_map/ppermute | solution.py:553
  109.8 6.4 %copy-start = (bf16[512,1024]{1,0:T(8,128)(2,1)S(1)}, bf16[512,1024]{1,0:T(8,128)(2,1)}, u32[]{:S(2)}) copy-start(bf16[512,1024]{1,0:T(8,128)(2,1)} %get-tuple-element.60.residual) | copy-start | bytes 3145732
  109.8 14.9 %collective-permute-start.22 = (bf16[256,1024]{1,0:T(8,128)(2,1)S(1)}, bf16[256,1024]{1,0:T(8,128)(2,1)S(1)}, u32[]{:S(2)}, u32[]{:S(2)}) collective-permute-start(bf16[256,1024]{1,0:T(8,128)(2,1)S(1)} %get-tuple-element.68), channel_id=1, source_target_pairs={{2,0},{3,1},{4,2},{5,3},{6,4},{7,5},{0,6},{1,7},{10,8},{11,9},{12,... | collective-permute-start | bytes 1572872 | tf_op jit(solution)/shard_map/ppermute | solution.py:553
  114.0 18.6 %collective-permute-start.16 = (bf16[256,1024]{1,0:T(8,128)(2,1)S(1)}, bf16[256,1024]{1,0:T(8,128)(2,1)S(1)}, u32[]{:S(2)}, u32[]{:S(2)}) collective-permute-start(bf16[256,1024]{1,0:T(8,128)(2,1)S(1)} %get-tuple-element.63), channel_id=1, source_target_pairs={{6,0},{7,1},{0,2},{1,3},{2,4},{3,5},{4,6},{5,7},{14,8},{15,9},{8,1... | collective-permute-start | bytes 1572872 | tf_op jit(solution)/shard_map/ppermute | solution.py:553
  115.4 18.6 %collective-permute-start.17 = (bf16[256,1024]{1,0:T(8,128)(2,1)S(1)}, bf16[256,1024]{1,0:T(8,128)(2,1)S(1)}, u32[]{:S(2)}, u32[]{:S(2)}) collective-permute-start(bf16[256,1024]{1,0:T(8,128)(2,1)S(1)} %get-tuple-element.64), channel_id=1, source_target_pairs={{2,0},{3,1},{4,2},{5,3},{6,4},{7,5},{0,6},{1,7},{10,8},{11,9},{12,... | collective-permute-start | bytes 1572872 | tf_op jit(solution)/shard_map/ppermute | solution.py:553

commit v3 on v2

--- a/solution.py
+++ b/solution.py
@@ -574,7 +574,7 @@
     far_second = [from_section(all_second, 0, k) for k in RING[:2]]
     near = [[(0, k)] for k in RING] + [[(k, 0)] for k in RING]
     table = cache_table(placement, section)
-    *state, cache = attention(
+    *state, cache, w_own, w_other = attention(
         queries,
         (first, second),
         row_first + row_second,
@@ -583,6 +583,7 @@
         diagonal=True,
         table=table,
         halves=[0] * 3 + [1] * 3,
+        staged=(out_weight, w_other),
     )
     all_first, all_second, *state = lax.optimization_barrier((all_first, all_second, *state))
     far_first.append(from_section(all_first, RING[2], 0))
@@ -600,7 +601,7 @@
     )
     pieces, plan = far_first[2:] + far_second[2:], far[0][2:] + far[1][2:]
     (early,) = attention(queries, state, pieces, plan, "attention_last", share=0)
-    late, cache, w_own, w_other = attention(
+    late, cache = attention(
         queries,
         state,
         pieces,
@@ -610,7 +611,6 @@
         table=table,
         cache=cache,
         halves=[0, 1],
-        staged=(out_weight, w_other),
     )
     mixed = []
     for share, own in enumerate((early, late)):

time: 135 us -> 125 us (0.926); the launches traced: 135 us -> 124 us
  waiting for transfers between devices: 38.7 us -> 28.4 us
  local copies, waits for them, and re-layouts: 1.33 us -> 4.7 us
  starting transfers between devices: 30.3 us -> 27 us
    ppermute x12, waiting for transfers between devices: 15.2 us -> 4.76 us  [from_section(): return lax.ppermute(value, 'section', pairs)]
    unnamed x16 -> x14, local copies, waits for them, and re-layouts: 1.06 us -> 4.44 us
    ppermute x12, starting transfers between devices: 21.2 us -> 17.9 us  [from_section(): return lax.ppermute(value, 'section', pairs)]
  transfers between devices with their start and end apart: 23 -> 23, of which waited for: 10 -> 10; matrix products, arithmetic and copies ran while one was open for 0% -> 0% of each run, Pallas kernels for 34% -> 36%
where the time goes in v3:
time: 125 us; the launch traced here: 124 us
  Pallas kernels  62.2 us (50%)
  waiting for transfers between devices  28.4 us (23%)
  starting transfers between devices  27 us (22%)
  local copies, waits for them, and re-layouts  4.7 us (4%)
    pallas_call x4, Pallas kernels, attention(): pl.pallas_call(functools.partial(attend_kernel, plan, halves, diagonal, f...  32.4 us
    ppermute x11, waiting for transfers between devices, from_tp(): return lax.ppermute(value, 'tp', pairs)  23.6 us
    ppermute x12, starting transfers between devices, from_section(): return lax.ppermute(value, 'section', pairs)  17.9 us
    pallas_call x1, Pallas kernels, norm_kv(): pl.pallas_call(norm_kv_kernel, in_specs=[ANY, WHOLE, ANY, WHOLE, WHOLE, W...  12.7 us
    pallas_call x1, Pallas kernels, query(): pl.pallas_call(query_kernel, in_specs=[ANY, WHOLE, WHOLE, ANY, WHOLE, WHO...  9.79 us
    ppermute x11, starting transfers between devices, from_tp(): return lax.ppermute(value, 'tp', pairs)  9.11 us
    pallas_call x6, Pallas kernels, project(): pl.pallas_call(kernel, in_specs=[WHOLE] * (len(terms) + len(extra)), out_...  5.42 us
    ppermute x12, waiting for transfers between devices, from_section(): return lax.ppermute(value, 'section', pairs)  4.76 us
  transfers between devices with their start and end apart: 23, of which 10 were waited for; matrix products, arithmetic and copies ran while one was open for 0% of the time, Pallas kernels for 36%

profile of v3, /device:TPU:14, one launch (start us, length us, event | category | flops | bytes accessed | tf_op | source)
XLA Modules:
  0.0 123.5 jit_solution(6028150146992225786)
XLA Ops:
  0.6 12.7 %norm_kv.1 = (f32[512,128]{1,0:T(8,128)}, bf16[256,256]{1,0:T(8,128)(2,1)}, bf16[256,256]{1,0:T(8,128)(2,1)}, bf16[512,1024]{1,0:T(8,128)(2,1)}, bf16[4,512,1024]{2,1,0:T(8,128)(2,1)}) custom-call(bf16[512,8192]{1,0:T(8,128)(2,1)} %tokens.3, f32[1,8192]{1,0:T(1,128)} %bitcast.3, bf16[8192,256]{1,0:T(8,128)(2,1)} %weight.2, f32[1,256]{1,0:T(1,128)} %bitcast.6, ...), custom_call_target="tpu_custom_call" | custom-call | flops 2147483648 | bytes 20971520 | tf_op jit(solution)/shard_map/norm_kv/pallas_call | solution.py:136
  13.3 0.1 collective-permute-start.1
  13.4 4.1 %collective-permute-start.2 = (bf16[256,256]{1,0:T(8,128)(2,1)}, bf16[256,256]{1,0:T(8,128)(2,1)S(1)}, u32[]{:S(2)}, u32[]{:S(2)}) collective-permute-start(bf16[256,256]{1,0:T(8,128)(2,1)} %get-tuple-element.36.refs_0_.refs_1_), channel_id=1, source_target_pairs={{8,0},{16,8},{24,16},{0,24},{40,32},{48,40},{56,48},{32,56},{72,64... | collective-permute-start | bytes 393224 | tf_op jit(solution)/shard_map/ppermute | solution.py:545
  17.5 0.0 collective-permute-start
  17.5 1.9 %collective-permute-start.3 = (bf16[256,256]{1,0:T(8,128)(2,1)}, bf16[256,256]{1,0:T(8,128)(2,1)S(1)}, u32[]{:S(2)}, u32[]{:S(2)}) collective-permute-start(bf16[256,256]{1,0:T(8,128)(2,1)} %get-tuple-element.36.refs_0_.refs_1_), channel_id=1, source_target_pairs={{16,0},{24,8},{0,16},{8,24},{48,32},{56,40},{32,48},{40,56},{80,64... | collective-permute-start | bytes 393224 | tf_op jit(solution)/shard_map/ppermute | solution.py:545
  19.4 0.8 collective-permute-start.4
  20.2 0.1 eq.32
  20.3 0.1 convert_reduce_fusion
  20.5 0.1 select_reduce_fusion
  20.6 0.6 collective-permute-done.2.refs_1_.refs_3_
  21.2 1.9 %collective-permute-start.5 = (bf16[256,256]{1,0:T(8,128)(2,1)}, bf16[256,256]{1,0:T(8,128)(2,1)S(1)}, u32[]{:S(2)}, u32[]{:S(2)}) collective-permute-start(bf16[256,256]{1,0:T(8,128)(2,1)} %get-tuple-element.43.refs_4_.refs_2_), channel_id=1, source_target_pairs={{96,0},{104,8},{112,16},{120,24},{0,32},{8,40},{16,48},{24,56},{32... | collective-permute-start | bytes 393224 | tf_op jit(solution)/shard_map/ppermute | solution.py:545
  23.1 4.2 %collective-permute-done.refs_2_.refs_4_ = bf16[256,256]{1,0:T(8,128)(2,1)S(1)} collective-permute-done((bf16[256,256]{1,0:T(8,128)(2,1)}, bf16[256,256]{1,0:T(8,128)(2,1)S(1)}, u32[]{:S(2)}, u32[]{:S(2)}) %collective-permute-start) | collective-permute-done | bytes 131104 | tf_op jit(solution)/shard_map/ppermute | solution.py:545
  27.3 1.4 %collective-permute-start.6 = (bf16[256,256]{1,0:T(8,128)(2,1)}, bf16[256,256]{1,0:T(8,128)(2,1)S(1)}, u32[]{:S(2)}, u32[]{:S(2)}) collective-permute-start(bf16[256,256]{1,0:T(8,128)(2,1)} %get-tuple-element.43.refs_4_.refs_2_), channel_id=1, source_target_pairs={{64,0},{72,8},{80,16},{88,24},{96,32},{104,40},{112,48},{120,56},{... | collective-permute-start | bytes 393224 | tf_op jit(solution)/shard_map/ppermute | solution.py:545
  28.7 9.8 %query.1.refs_0_ = bf16[2048,128]{1,0:T(8,128)(2,1)} custom-call(bf16[512,8192]{1,0:T(8,128)(2,1)} %tokens.3, f32[512,128]{1,0:T(8,128)} %get-tuple-element.39.factors, f32[1,8192]{1,0:T(1,128)} %bitcast.4, bf16[8192,512]{1,0:T(8,128)(2,1)} %weight.3, f32[1,512]{1,0:T(1,128)} %bitcast.5, f32[512,256]{1,0:T(8,128)} %constant.17.clone.small, ...), custom_call_target="tpu_custom_call" | custom-call | flops 4294967296 | bytes 16777216 | tf_op jit(solution)/shard_map/query/pallas_call | solution.py:217
  38.5 0.0 collective-permute-done.1.refs_11_
  38.5 0.0 collective-permute-done.3.refs_3_.refs_5_
  38.5 0.0 collective-permute-done.4.refs_5_.refs_6_
  38.6 0.0 collective-permute-done.6.refs_7_.refs_8_
  38.6 0.1 join.1
  38.7 0.1 collective-permute-start.7
  38.7 3.2 %collective-permute-start.8 = (bf16[1024,256]{1,0:T(8,128)(2,1)S(1)}, bf16[1024,256]{1,0:T(8,128)(2,1)S(1)}, u32[]{:S(2)}, u32[]{:S(2)}) collective-permute-start(bf16[1024,256]{1,0:T(8,128)(2,1)S(1)} %get-tuple-element.54), channel_id=1, source_target_pairs={{96,0},{104,8},{112,16},{120,24},{0,32},{8,40},{16,48},{24,56},{32... | collective-permute-start | bytes 1572872 | tf_op jit(solution)/shard_map/ppermute | solution.py:545
  42.0 0.0 collective-permute-start.10
  42.0 3.2 %collective-permute-start.9 = (bf16[1024,256]{1,0:T(8,128)(2,1)S(1)}, bf16[1024,256]{1,0:T(8,128)(2,1)}, u32[]{:S(2)}, u32[]{:S(2)}) collective-permute-start(bf16[1024,256]{1,0:T(8,128)(2,1)S(1)} %get-tuple-element.55), channel_id=1, source_target_pairs={{8,0},{16,8},{24,16},{0,24},{40,32},{48,40},{56,48},{32,56},{72,64... | collective-permute-start | bytes 1572872 | tf_op jit(solution)/shard_map/ppermute | solution.py:545
  45.2 0.1 copy.13
  45.3 0.1 sub.7.refs_9_.refs_7_.refs_5_
  45.4 0.0 copy-start
  45.4 3.4 %copy-done = bf16[512,8192]{1,0:T(8,128)(2,1)S(1)} copy-done((bf16[512,8192]{1,0:T(8,128)(2,1)S(1)}, bf16[512,8192]{1,0:T(8,128)(2,1)}, u32[]{:S(2)}) %copy-start) | copy-done | bytes 8388632
  48.8 1.0 copy-done.2
  49.8 7.4 %attention_near.1 = (f32[2048,256]{1,0:T(8,128)S(1)}, f32[2048,128]{1,0:T(8,128)S(1)}, bf16[64,16,256]{2,1,0:T(8,128)(2,1)S(1)}, bf16[4,512,1024]{2,1,0:T(8,128)(2,1)S(1)}, bf16[4,512,1024]{2,1,0:T(8,128)(2,1)S(1)}) custom-call(bf16[2048,128]{1,0:T(8,128)(2,1)S(1)} %copy-done.2, bf16[256,256]{1,0:T(8,128)(2,1)S(1)} %copy-done.4, ...), custom_call_target="tpu_custom_call" | custom-call | flops 5368709120 | bytes 8388608 | tf_op jit(solution)/shard_map/attention_near/pallas_call | solution.py:433
  57.2 1.1 collective-permute-start.11
  58.3 0.1 collective-permute-start.12
  58.4 0.0 collective-permute-done.9.refs_5_
  58.4 14.7 %attention_far.1 = (f32[2048,256]{1,0:T(8,128)S(1)}, f32[2048,128]{1,0:T(8,128)S(1)}, bf16[64,16,256]{2,1,0:T(8,128)(2,1)S(1)}) custom-call(bf16[2048,128]{1,0:T(8,128)(2,1)S(1)} %copy-done.3, f32[2048,256]{1,0:T(8,128)S(1)} %get-tuple-element.49.refs_1_, f32[2048,128]{1,0:T(8,128)S(1)} %get-tuple-element.50.refs_2_, ...), custom_call_target="tpu_custom_call" | custom-call | flops 8589934592 | bytes 8388608 | tf_op jit(solution)/shard_map/attention_far/pallas_call | solution.py:433
  73.1 0.0 collective-permute-done.11.refs_3_
  73.1 4.2 %attention_last.3.own = bf16[256,512]{1,0:T(8,128)(2,1)S(1)} custom-call(bf16[2048,128]{1,0:T(8,128)(2,1)S(1)} %copy-done.3, f32[2048,256]{1,0:T(8,128)S(1)} %get-tuple-element.52.refs_1_, f32[2048,128]{1,0:T(8,128)S(1)} %get-tuple-element.53.refs_2_, bf16[1024,256]{1,0:T(8,128)(2,1)S(1)} %collective-permute-done.11.refs_3_, ...), custom_call_target="tpu_custom_call" | custom-call | flops 2147483648 | bytes 8388608 | tf_op jit(solution)/shard_map/attention_last/pallas_call | solution.py:433
  77.3 0.1 collective-permute-start.18
  77.4 6.2 %attention_last.2 = (bf16[256,512]{1,0:T(8,128)(2,1)S(1)}, bf16[64,16,256]{2,1,0:T(8,128)(2,1)}) custom-call(bf16[2048,128]{1,0:T(8,128)(2,1)S(1)} %copy-done.3, f32[2048,256]{1,0:T(8,128)S(1)} %get-tuple-element.52.refs_1_, f32[2048,128]{1,0:T(8,128)S(1)} %get-tuple-element.53.refs_2_, bf16[1024,256]{1,0:T(8,128)(2,1)S(1)} %collective-permute-done.11.refs_3_, ...), custom_call_target="tpu_custom_call" | custom-call | flops 2147483648 | bytes 8388608 | tf_op jit(solution)/shard_map/attention_last/pallas_call | solution.py:433
  83.6 0.6 collective-permute-start.13
  84.1 0.0 collective-permute-done.18.other
  84.1 0.7 project_opposite.3
  84.9 1.6 %collective-permute-start.19 = (bf16[128,1024]{1,0:T(8,128)(2,1)S(1)}, bf16[128,1024]{1,0:T(8,128)(2,1)S(1)}, u32[]{:S(2)}, u32[]{:S(2)}) collective-permute-start(bf16[128,1024]{1,0:T(8,128)(2,1)S(1)} %get-tuple-element.65), channel_id=1, source_target_pairs={{6,0},{7,1},{0,2},{1,3},{2,4},{3,5},{4,6},{5,7},{14,8},{15,9},{8,1... | collective-permute-start | bytes 786440 | tf_op jit(solution)/shard_map/ppermute | solution.py:553
  86.5 0.5 collective-permute-start.20
  87.0 0.0 collective-permute-done.13.other
  87.0 0.7 project_opposite.2
  87.7 1.6 %collective-permute-start.14 = (bf16[128,1024]{1,0:T(8,128)(2,1)S(1)}, bf16[128,1024]{1,0:T(8,128)(2,1)S(1)}, u32[]{:S(2)}, u32[]{:S(2)}) collective-permute-start(bf16[128,1024]{1,0:T(8,128)(2,1)S(1)} %get-tuple-element.61), channel_id=1, source_target_pairs={{6,0},{7,1},{0,2},{1,3},{2,4},{3,5},{4,6},{5,7},{14,8},{15,9},{8,1... | collective-permute-start | bytes 786440 | tf_op jit(solution)/shard_map/ppermute | solution.py:553
  89.3 0.5 collective-permute-start.15
  89.8 4.3 %collective-permute-done.19.from_below = bf16[128,1024]{1,0:T(8,128)(2,1)S(1)} collective-permute-done((bf16[128,1024]{1,0:T(8,128)(2,1)S(1)}, bf16[128,1024]{1,0:T(8,128)(2,1)S(1)}, u32[]{:S(2)}, u32[]{:S(2)}) %collective-permute-start.19) | collective-permute-done | bytes 262176 | tf_op jit(solution)/shard_map/ppermute | solution.py:553
  94.1 1.6 %collective-permute-done.20.from_above = bf16[128,1024]{1,0:T(8,128)(2,1)S(1)} collective-permute-done((bf16[128,1024]{1,0:T(8,128)(2,1)S(1)}, bf16[128,1024]{1,0:T(8,128)(2,1)S(1)}, u32[]{:S(2)}, u32[]{:S(2)}) %collective-permute-start.20) | collective-permute-done | bytes 262176 | tf_op jit(solution)/shard_map/ppermute | solution.py:553
  95.7 1.3 %project_neighbours.3 = (bf16[256,1024]{1,0:T(8,128)(2,1)S(1)}, bf16[256,1024]{1,0:T(8,128)(2,1)S(1)}) custom-call(bf16[256,512]{1,0:T(8,128)(2,1)S(1)} %attention_last.3.own, bf16[256,512]{1,0:T(8,128)(2,1)S(1)} %collective-permute-done.18.other, bf16[4,512,1024]{2,1,0:T(8,128)(2,1)S(1)} %get-tuple-element.58.w_own, ...), custom_call_target="tpu_custom_call" | custom-call | flops 1073741824 | bytes 4194304 | tf_op jit(solution)/shard_map/project_neighbours/pallas_call | solution.py:509
  97.0 1.4 %collective-permute-start.21 = (bf16[256,1024]{1,0:T(8,128)(2,1)S(1)}, bf16[256,1024]{1,0:T(8,128)(2,1)S(1)}, u32[]{:S(2)}, u32[]{:S(2)}) collective-permute-start(bf16[256,1024]{1,0:T(8,128)(2,1)S(1)} %get-tuple-element.67), channel_id=1, source_target_pairs={{6,0},{7,1},{0,2},{1,3},{2,4},{3,5},{4,6},{5,7},{14,8},{15,9},{8,1... | collective-permute-start | bytes 1572872 | tf_op jit(solution)/shard_map/ppermute | solution.py:553
  98.3 0.7 collective-permute-start.22
  99.1 0.6 collective-permute-done.14.from_below
  99.7 1.6 %collective-permute-done.15.from_above = bf16[128,1024]{1,0:T(8,128)(2,1)S(1)} collective-permute-done((bf16[128,1024]{1,0:T(8,128)(2,1)S(1)}, bf16[128,1024]{1,0:T(8,128)(2,1)S(1)}, u32[]{:S(2)}, u32[]{:S(2)}) %collective-permute-start.15) | collective-permute-done | bytes 262176 | tf_op jit(solution)/shard_map/ppermute | solution.py:553
  101.3 1.3 %project_neighbours.2 = (bf16[256,1024]{1,0:T(8,128)(2,1)S(1)}, bf16[256,1024]{1,0:T(8,128)(2,1)S(1)}) custom-call(bf16[256,512]{1,0:T(8,128)(2,1)S(1)} %get-tuple-element.57.own, bf16[256,512]{1,0:T(8,128)(2,1)S(1)} %collective-permute-done.13.other, bf16[4,512,1024]{2,1,0:T(8,128)(2,1)S(1)} %get-tuple-element.58.w_own, ...), custom_call_target="tpu_custom_call" | custom-call | flops 1073741824 | bytes 4194304 | tf_op jit(solution)/shard_map/project_neighbours/pallas_call | solution.py:509
  102.6 1.4 %collective-permute-start.16 = (bf16[256,1024]{1,0:T(8,128)(2,1)S(1)}, bf16[256,1024]{1,0:T(8,128)(2,1)S(1)}, u32[]{:S(2)}, u32[]{:S(2)}) collective-permute-start(bf16[256,1024]{1,0:T(8,128)(2,1)S(1)} %get-tuple-element.63), channel_id=1, source_target_pairs={{6,0},{7,1},{0,2},{1,3},{2,4},{3,5},{4,6},{5,7},{14,8},{15,9},{8,1... | collective-permute-start | bytes 1572872 | tf_op jit(solution)/shard_map/ppermute | solution.py:553
  104.0 0.7 collective-permute-start.17
  104.7 0.7 project_home.3.base
  105.4 0.7 project_home.2.base
  106.2 5.7 %collective-permute-done.21.from_below = bf16[256,1024]{1,0:T(8,128)(2,1)S(1)} collective-permute-done((bf16[256,1024]{1,0:T(8,128)(2,1)S(1)}, bf16[256,1024]{1,0:T(8,128)(2,1)S(1)}, u32[]{:S(2)}, u32[]{:S(2)}) %collective-permute-start.21) | collective-permute-done | bytes 524320 | tf_op jit(solution)/shard_map/ppermute | solution.py:553
  111.9 1.3 %collective-permute-done.22.from_above = bf16[256,1024]{1,0:T(8,128)(2,1)S(1)} collective-permute-done((bf16[256,1024]{1,0:T(8,128)(2,1)S(1)}, bf16[256,1024]{1,0:T(8,128)(2,1)S(1)}, u32[]{:S(2)}, u32[]{:S(2)}) %collective-permute-start.22) | collective-permute-done | bytes 524320 | tf_op jit(solution)/shard_map/ppermute | solution.py:553
  113.2 0.9 finish.2.refs_0_
  114.1 7.1 %collective-permute-done.16.from_below = bf16[256,1024]{1,0:T(8,128)(2,1)S(1)} collective-permute-done((bf16[256,1024]{1,0:T(8,128)(2,1)S(1)}, bf16[256,1024]{1,0:T(8,128)(2,1)S(1)}, u32[]{:S(2)}, u32[]{:S(2)}) %collective-permute-start.16) | collective-permute-done | bytes 524320 | tf_op jit(solution)/shard_map/ppermute | solution.py:553
  121.3 1.3 %collective-permute-done.17.from_above = bf16[256,1024]{1,0:T(8,128)(2,1)S(1)} collective-permute-done((bf16[256,1024]{1,0:T(8,128)(2,1)S(1)}, bf16[256,1024]{1,0:T(8,128)(2,1)S(1)}, u32[]{:S(2)}, u32[]{:S(2)}) %collective-permute-start.17) | collective-permute-done | bytes 524320 | tf_op jit(solution)/shard_map/ppermute | solution.py:553
  122.6 0.9 finish.3
  (20 shorter events, 0.1 us)
Async XLA Ops:
  0.6 19.6 %copy-start.6 = (s32[512,1]{0,1:T(1,128)S(1)}, s32[512,1]{0,1:T(1,128)}, u32[]{:S(2)}) copy-start(s32[512,1]{0,1:T(1,128)} %param.17) | copy-start | bytes 6148
  13.3 25.2 %collective-permute-start.1 = (bf16[4,512,1024]{2,1,0:T(8,128)(2,1)}, bf16[4,512,1024]{2,1,0:T(8,128)(2,1)}, u32[]{:S(2)}, u32[]{:S(2)}) collective-permute-start(bf16[4,512,1024]{2,1,0:T(8,128)(2,1)} %get-tuple-element.37), channel_id=1, source_target_pairs={{1,0},{0,1},{3,2},{2,3},{5,4},{4,5},{7,6},{6,7},{9,8},{8,9},{11,10... | collective-permute-start | bytes 12582920 | tf_op jit(solution)/shard_map/ppermute | solution.py:553
  13.4 7.8 %collective-permute-start.2 = (bf16[256,256]{1,0:T(8,128)(2,1)}, bf16[256,256]{1,0:T(8,128)(2,1)S(1)}, u32[]{:S(2)}, u32[]{:S(2)}) collective-permute-start(bf16[256,256]{1,0:T(8,128)(2,1)} %get-tuple-element.36.refs_0_.refs_1_), channel_id=1, source_target_pairs={{8,0},{16,8},{24,16},{0,24},{40,32},{48,40},{56,48},{32,56},{72,64... | collective-permute-start | bytes 393224 | tf_op jit(solution)/shard_map/ppermute | solution.py:545
  17.5 9.8 %collective-permute-start = (bf16[256,256]{1,0:T(8,128)(2,1)}, bf16[256,256]{1,0:T(8,128)(2,1)S(1)}, u32[]{:S(2)}, u32[]{:S(2)}) collective-permute-start(bf16[256,256]{1,0:T(8,128)(2,1)} %get-tuple-element.36.refs_0_.refs_1_), channel_id=1, source_target_pairs={{24,0},{0,8},{8,16},{16,24},{56,32},{32,40},{40,48},{48,56},{88,64... | collective-permute-start | bytes 393224 | tf_op jit(solution)/shard_map/ppermute | solution.py:545
  17.5 21.0 %collective-permute-start.3 = (bf16[256,256]{1,0:T(8,128)(2,1)}, bf16[256,256]{1,0:T(8,128)(2,1)S(1)}, u32[]{:S(2)}, u32[]{:S(2)}) collective-permute-start(bf16[256,256]{1,0:T(8,128)(2,1)} %get-tuple-element.36.refs_0_.refs_1_), channel_id=1, source_target_pairs={{16,0},{24,8},{0,16},{8,24},{48,32},{56,40},{32,48},{40,56},{80,64... | collective-permute-start | bytes 393224 | tf_op jit(solution)/shard_map/ppermute | solution.py:545
  19.4 19.2 %collective-permute-start.4 = (bf16[256,256]{1,0:T(8,128)(2,1)}, bf16[256,256]{1,0:T(8,128)(2,1)S(1)}, u32[]{:S(2)}, u32[]{:S(2)}) collective-permute-start(bf16[256,256]{1,0:T(8,128)(2,1)} %get-tuple-element.43.refs_4_.refs_2_), channel_id=1, source_target_pairs={{32,0},{40,8},{48,16},{56,24},{64,32},{72,40},{80,48},{88,56},{96,... | collective-permute-start | bytes 393224 | tf_op jit(solution)/shard_map/ppermute | solution.py:545
  21.2 17.4 %collective-permute-start.5 = (bf16[256,256]{1,0:T(8,128)(2,1)}, bf16[256,256]{1,0:T(8,128)(2,1)S(1)}, u32[]{:S(2)}, u32[]{:S(2)}) collective-permute-start(bf16[256,256]{1,0:T(8,128)(2,1)} %get-tuple-element.43.refs_4_.refs_2_), channel_id=1, source_target_pairs={{96,0},{104,8},{112,16},{120,24},{0,32},{8,40},{16,48},{24,56},{32... | collective-permute-start | bytes 393224 | tf_op jit(solution)/shard_map/ppermute | solution.py:545
  27.3 11.2 %collective-permute-start.6 = (bf16[256,256]{1,0:T(8,128)(2,1)}, bf16[256,256]{1,0:T(8,128)(2,1)S(1)}, u32[]{:S(2)}, u32[]{:S(2)}) collective-permute-start(bf16[256,256]{1,0:T(8,128)(2,1)} %get-tuple-element.43.refs_4_.refs_2_), channel_id=1, source_target_pairs={{64,0},{72,8},{80,16},{88,24},{96,32},{104,40},{112,48},{120,56},{... | collective-permute-start | bytes 393224 | tf_op jit(solution)/shard_map/ppermute | solution.py:545
  28.7 9.9 %copy-start.4 = (bf16[256,256]{1,0:T(8,128)(2,1)S(1)}, bf16[256,256]{1,0:T(8,128)(2,1)}, u32[]{:S(2)}) copy-start(bf16[256,256]{1,0:T(8,128)(2,1)} %get-tuple-element.36.refs_0_.refs_1_) | copy-start | bytes 393220
  28.7 9.9 %copy-start.5 = (bf16[256,256]{1,0:T(8,128)(2,1)S(1)}, bf16[256,256]{1,0:T(8,128)(2,1)}, u32[]{:S(2)}) copy-start(bf16[256,256]{1,0:T(8,128)(2,1)} %get-tuple-element.43.refs_4_.refs_2_) | copy-start | bytes 393220
  38.7 19.7 %collective-permute-start.7 = (bf16[1024,256]{1,0:T(8,128)(2,1)S(1)}, bf16[1024,256]{1,0:T(8,128)(2,1)S(1)}, u32[]{:S(2)}, u32[]{:S(2)}) collective-permute-start(bf16[1024,256]{1,0:T(8,128)(2,1)S(1)} %get-tuple-element.54), channel_id=1, source_target_pairs={{32,0},{40,8},{48,16},{56,24},{64,32},{72,40},{80,48},{88,56},{96,... | collective-permute-start | bytes 1572872 | tf_op jit(solution)/shard_map/ppermute | solution.py:545
  38.7 19.6 %collective-permute-start.8 = (bf16[1024,256]{1,0:T(8,128)(2,1)S(1)}, bf16[1024,256]{1,0:T(8,128)(2,1)S(1)}, u32[]{:S(2)}, u32[]{:S(2)}) collective-permute-start(bf16[1024,256]{1,0:T(8,128)(2,1)S(1)} %get-tuple-element.54), channel_id=1, source_target_pairs={{96,0},{104,8},{112,16},{120,24},{0,32},{8,40},{16,48},{24,56},{32... | collective-permute-start | bytes 1572872 | tf_op jit(solution)/shard_map/ppermute | solution.py:545
  42.0 16.3 %collective-permute-start.10 = (bf16[1024,256]{1,0:T(8,128)(2,1)S(1)}, bf16[1024,256]{1,0:T(8,128)(2,1)}, u32[]{:S(2)}, u32[]{:S(2)}) collective-permute-start(bf16[1024,256]{1,0:T(8,128)(2,1)S(1)} %get-tuple-element.55), channel_id=1, source_target_pairs={{24,0},{0,8},{8,16},{16,24},{56,32},{32,40},{40,48},{48,56},{88,64... | collective-permute-start | bytes 1572872 | tf_op jit(solution)/shard_map/ppermute | solution.py:545
  42.0 16.4 %collective-permute-start.9 = (bf16[1024,256]{1,0:T(8,128)(2,1)S(1)}, bf16[1024,256]{1,0:T(8,128)(2,1)}, u32[]{:S(2)}, u32[]{:S(2)}) collective-permute-start(bf16[1024,256]{1,0:T(8,128)(2,1)S(1)} %get-tuple-element.55), channel_id=1, source_target_pairs={{8,0},{16,8},{24,16},{0,24},{40,32},{48,40},{56,48},{32,56},{72,64... | collective-permute-start | bytes 1572872 | tf_op jit(solution)/shard_map/ppermute | solution.py:545
  45.4 3.4 %copy-start = (bf16[512,8192]{1,0:T(8,128)(2,1)S(1)}, bf16[512,8192]{1,0:T(8,128)(2,1)}, u32[]{:S(2)}) copy-start(bf16[512,8192]{1,0:T(8,128)(2,1)} %refs_10_.1) | copy-start | bytes 25165828
  48.8 1.0 copy-start.2
  49.8 8.6 %copy-start.3 = (bf16[2048,128]{1,0:T(8,128)(2,1)S(1)}, bf16[2048,128]{1,0:T(8,128)(2,1)}, u32[]{:S(2)}) copy-start(bf16[2048,128]{1,0:T(8,128)(2,1)} %query.1.refs_0_) | copy-start | bytes 1572868
  57.2 15.9 %collective-permute-start.11 = (bf16[1024,256]{1,0:T(8,128)(2,1)S(1)}, bf16[1024,256]{1,0:T(8,128)(2,1)S(1)}, u32[]{:S(2)}, u32[]{:S(2)}) collective-permute-start(bf16[1024,256]{1,0:T(8,128)(2,1)S(1)} %get-tuple-element.54), channel_id=1, source_target_pairs={{64,0},{72,8},{80,16},{88,24},{96,32},{104,40},{112,48},{120,56},{... | collective-permute-start | bytes 1572872 | tf_op jit(solution)/shard_map/ppermute | solution.py:545
  58.3 14.8 %collective-permute-start.12 = (bf16[1024,256]{1,0:T(8,128)(2,1)S(1)}, bf16[1024,256]{1,0:T(8,128)(2,1)S(1)}, u32[]{:S(2)}, u32[]{:S(2)}) collective-permute-start(bf16[1024,256]{1,0:T(8,128)(2,1)S(1)} %get-tuple-element.55), channel_id=1, source_target_pairs={{16,0},{24,8},{0,16},{8,24},{48,32},{56,40},{32,48},{40,56},{80,64... | collective-permute-start | bytes 1572872 | tf_op jit(solution)/shard_map/ppermute | solution.py:545
  77.3 6.8 %collective-permute-start.18 = (bf16[256,512]{1,0:T(8,128)(2,1)S(1)}, bf16[256,512]{1,0:T(8,128)(2,1)S(1)}, u32[]{:S(2)}, u32[]{:S(2)}) collective-permute-start(bf16[256,512]{1,0:T(8,128)(2,1)S(1)} %attention_last.3.own), channel_id=1, source_target_pairs={{1,0},{0,1},{3,2},{2,3},{5,4},{4,5},{7,6},{6,7},{9,8},{8,9},{11,10... | collective-permute-start | bytes 786440 | tf_op jit(solution)/shard_map/ppermute | solution.py:553
  83.6 3.4 %collective-permute-start.13 = (bf16[256,512]{1,0:T(8,128)(2,1)S(1)}, bf16[256,512]{1,0:T(8,128)(2,1)S(1)}, u32[]{:S(2)}, u32[]{:S(2)}) collective-permute-start(bf16[256,512]{1,0:T(8,128)(2,1)S(1)} %get-tuple-element.57.own), channel_id=1, source_target_pairs={{1,0},{0,1},{3,2},{2,3},{5,4},{4,5},{7,6},{6,7},{9,8},{8,9},{11,10... | collective-permute-start | bytes 786440 | tf_op jit(solution)/shard_map/ppermute | solution.py:553
  84.9 9.2 %collective-permute-start.19 = (bf16[128,1024]{1,0:T(8,128)(2,1)S(1)}, bf16[128,1024]{1,0:T(8,128)(2,1)S(1)}, u32[]{:S(2)}, u32[]{:S(2)}) collective-permute-start(bf16[128,1024]{1,0:T(8,128)(2,1)S(1)} %get-tuple-element.65), channel_id=1, source_target_pairs={{6,0},{7,1},{0,2},{1,3},{2,4},{3,5},{4,6},{5,7},{14,8},{15,9},{8,1... | collective-permute-start | bytes 786440 | tf_op jit(solution)/shard_map/ppermute | solution.py:553
  86.5 9.2 %collective-permute-start.20 = (bf16[128,1024]{1,0:T(8,128)(2,1)S(1)}, bf16[128,1024]{1,0:T(8,128)(2,1)S(1)}, u32[]{:S(2)}, u32[]{:S(2)}) collective-permute-start(bf16[128,1024]{1,0:T(8,128)(2,1)S(1)} %get-tuple-element.66), channel_id=1, source_target_pairs={{2,0},{3,1},{4,2},{5,3},{6,4},{7,5},{0,6},{1,7},{10,8},{11,9},{12,... | collective-permute-start | bytes 786440 | tf_op jit(solution)/shard_map/ppermute | solution.py:553
  87.7 12.0 %collective-permute-start.14 = (bf16[128,1024]{1,0:T(8,128)(2,1)S(1)}, bf16[128,1024]{1,0:T(8,128)(2,1)S(1)}, u32[]{:S(2)}, u32[]{:S(2)}) collective-permute-start(bf16[128,1024]{1,0:T(8,128)(2,1)S(1)} %get-tuple-element.61), channel_id=1, source_target_pairs={{6,0},{7,1},{0,2},{1,3},{2,4},{3,5},{4,6},{5,7},{14,8},{15,9},{8,1... | collective-permute-start | bytes 786440 | tf_op jit(solution)/shard_map/ppermute | solution.py:553
  89.3 12.0 %collective-permute-start.15 = (bf16[128,1024]{1,0:T(8,128)(2,1)S(1)}, bf16[128,1024]{1,0:T(8,128)(2,1)S(1)}, u32[]{:S(2)}, u32[]{:S(2)}) collective-permute-start(bf16[128,1024]{1,0:T(8,128)(2,1)S(1)} %get-tuple-element.62), channel_id=1, source_target_pairs={{2,0},{3,1},{4,2},{5,3},{6,4},{7,5},{0,6},{1,7},{10,8},{11,9},{12,... | collective-permute-start | bytes 786440 | tf_op jit(solution)/shard_map/ppermute | solution.py:553
  97.0 14.9 %collective-permute-start.21 = (bf16[256,1024]{1,0:T(8,128)(2,1)S(1)}, bf16[256,1024]{1,0:T(8,128)(2,1)S(1)}, u32[]{:S(2)}, u32[]{:S(2)}) collective-permute-start(bf16[256,1024]{1,0:T(8,128)(2,1)S(1)} %get-tuple-element.67), channel_id=1, source_target_pairs={{6,0},{7,1},{0,2},{1,3},{2,4},{3,5},{4,6},{5,7},{14,8},{15,9},{8,1... | collective-permute-start | bytes 1572872 | tf_op jit(solution)/shard_map/ppermute | solution.py:553
  98.3 6.4 %copy-start.1 = (bf16[512,1024]{1,0:T(8,128)(2,1)S(1)}, bf16[512,1024]{1,0:T(8,128)(2,1)}, u32[]{:S(2)}) copy-start(bf16[512,1024]{1,0:T(8,128)(2,1)} %get-tuple-element.60.residual) | copy-start | bytes 3145732
  98.3 14.9 %collective-permute-start.22 = (bf16[256,1024]{1,0:T(8,128)(2,1)S(1)}, bf16[256,1024]{1,0:T(8,128)(2,1)S(1)}, u32[]{:S(2)}, u32[]{:S(2)}) collective-permute-start(bf16[256,1024]{1,0:T(8,128)(2,1)S(1)} %get-tuple-element.68), channel_id=1, source_target_pairs={{2,0},{3,1},{4,2},{5,3},{6,4},{7,5},{0,6},{1,7},{10,8},{11,9},{12,... | collective-permute-start | bytes 1572872 | tf_op jit(solution)/shard_map/ppermute | solution.py:553
  102.6 18.6 %collective-permute-start.16 = (bf16[256,1024]{1,0:T(8,128)(2,1)S(1)}, bf16[256,1024]{1,0:T(8,128)(2,1)S(1)}, u32[]{:S(2)}, u32[]{:S(2)}) collective-permute-start(bf16[256,1024]{1,0:T(8,128)(2,1)S(1)} %get-tuple-element.63), channel_id=1, source_target_pairs={{6,0},{7,1},{0,2},{1,3},{2,4},{3,5},{4,6},{5,7},{14,8},{15,9},{8,1... | collective-permute-start | bytes 1572872 | tf_op jit(solution)/shard_map/ppermute | solution.py:553
  104.0 18.6 %collective-permute-start.17 = (bf16[256,1024]{1,0:T(8,128)(2,1)S(1)}, bf16[256,1024]{1,0:T(8,128)(2,1)S(1)}, u32[]{:S(2)}, u32[]{:S(2)}) collective-permute-start(bf16[256,1024]{1,0:T(8,128)(2,1)S(1)} %get-tuple-element.64), channel_id=1, source_target_pairs={{2,0},{3,1},{4,2},{5,3},{6,4},{7,5},{0,6},{1,7},{10,8},{11,9},{12,... | collective-permute-start | bytes 1572872 | tf_op jit(solution)/shard_map/ppermute | solution.py:553
